TPU v7x, 128 devices: a whole 4x4x4 slice. The times are simulated.
128 devices in a mesh: rows: 128 (over x, z, y, core).
Axes of the slice: x: 4, y: 4, z: 4, core: 2. Of those that a mesh axis runs over, the one named last changes fastest.
Arguments:
- order: int32 [1152], replicated, may hold values from 0 to 1151, as said below
- ham_cols: int32 [1152, 8], P('rows'), may hold values from -1 to 1151, as said below
- dens_cols: int32 [1152, 16], replicated, may hold values from -1 to 1151, as said below
- ham_blocks: bfloat16 [1152, 8, 128, 128], P('rows'), may hold values from -0.125 to 0.125
- coefficients: float32 [4], replicated, may hold values from 0.5 to 1.5
Outputs:
- fermi_blocks: float32 [1152, 16, 128, 128], P('rows')
Inputs may be any that keep to these rules, and one draw needn't show every extreme that they name: `order`: a permutation of the block-row ids. `ham_cols`: entries of a row are distinct; each names the block row at a spatial position within 4 of the row's own, or is -1 where that position lies beyond the ends. `dens_cols`: entries of a row are distinct; each names the block row at a spatial position within 9 of the row's own, or is -1 where that position lies beyond the ends.
All inputs are finite; a program needn't handle non-finite values.
Results may differ from a plain program's by a relative error of at most 0.0022.
Values may be sent and summed in bfloat16 or wider, within the bound.
No kernel may reach another device: no remote copies, remote signals or barrier semaphores. Data moves between devices by JAX's collectives and lax.ppermute only.
A program may use at most 320 MiB of HBM per device.

v0:
```python
import jax
import jax.numpy as jnp
from jax import lax
from jax.sharding import PartitionSpec as P

TERMS = 4
REACH = 4
PREACH = 9


def from_behind(block, axis, distance):
    devices = range(lax.axis_size(axis))
    route = [(i - distance, i) for i in devices if i - distance in devices]
    return lax.ppermute(block, axis, route)


def offset_maps(row_ham_cols, row_cols, ham_pos, dens_pos, inverse):
    ham_span = 2 * REACH + 1
    dens_span = 2 * PREACH + 1
    valid = row_ham_cols >= 0
    ham_offsets = inverse[jnp.maximum(row_ham_cols, 0)] - ham_pos[:, None]
    ham_onehot = (
        (ham_offsets[:, :, None] == (jnp.arange(ham_span, dtype=jnp.int32) - REACH)[None, None, :])
        & valid[:, :, None]
    ).astype(jnp.bfloat16)
    live = row_cols >= 0
    dens_offsets = inverse[jnp.maximum(row_cols, 0)] - dens_pos[:, None]
    dens_pick = (
        (
            dens_offsets[:, :, None]
            == (jnp.arange(dens_span, dtype=jnp.int32) - PREACH)[None, None, :]
        )
        & live[:, :, None]
    ).astype(jnp.float32)
    pattern = jnp.max(dens_pick, axis=1)
    return (ham_onehot, dens_pick, pattern)


def first_terms(ham_onehot, ham_rows, pattern, block_size):
    ham_span = 2 * REACH + 1
    dens_span = 2 * PREACH + 1
    by_offset = jnp.einsum(
        "pbd,pbxy->dpxy", ham_onehot, ham_rows, preferred_element_type=jnp.float32
    ).astype(jnp.bfloat16)
    place = (
        jnp.arange(ham_span, dtype=jnp.int32)[:, None] - REACH + PREACH
        == jnp.arange(dens_span, dtype=jnp.int32)[None, :]
    ).astype(jnp.bfloat16)
    cheb_one = (
        jnp.einsum("dpxy,de->pxey", by_offset, place, preferred_element_type=jnp.float32)
        * pattern[:, None, :, None]
    )
    centre = (jnp.arange(dens_span) == PREACH).astype(jnp.float32)
    cheb_zero = (
        jnp.eye(block_size, dtype=jnp.float32)[None, :, None, :]
        * centre[None, None, :, None]
        * pattern[:, None, :, None]
    )
    return (by_offset, cheb_zero, cheb_one)


def apply_ham(window, start, by_offset, count):
    block_size = window.shape[1]
    dens_span = window.shape[2]
    slots = 2 * REACH + 1
    left_rows = jnp.transpose(by_offset, (1, 2, 0, 3)).reshape(
        count, block_size, slots * block_size
    )

    def one_row(items):
        row_left, index = items
        nearby = lax.dynamic_slice_in_dim(window, start + index - REACH, slots, 0)
        pieces = []
        for slot in range(slots):
            step = slot - REACH
            piece = nearby[slot]
            if step > 0:
                piece = jnp.pad(piece[:, : dens_span - step], ((0, 0), (step, 0), (0, 0)))
            elif step < 0:
                piece = jnp.pad(piece[:, -step:], ((0, 0), (0, -step), (0, 0)))
            pieces.append(piece.reshape(block_size, dens_span * block_size))
        stacked = jnp.concatenate(pieces, axis=0)
        return jnp.dot(row_left, stacked, preferred_element_type=jnp.float32).reshape(
            block_size, dens_span, block_size
        )

    return lax.map(one_row, (left_rows, jnp.arange(count, dtype=jnp.int32)))


def to_slots(fermi, dens_pick):
    return jnp.einsum(
        "pae,pxez->paxz",
        dens_pick,
        fermi,
        precision=lax.Precision.HIGHEST,
        preferred_element_type=jnp.float32,
    )


def local(order, ham_cols, dens_cols, ham_blocks, coefficients):
    rows_here = ham_cols.shape[0]
    total_rows = order.shape[0]
    block_size = ham_blocks.shape[2]
    first_row = lax.axis_index("rows") * rows_here
    inverse = (
        jnp.zeros((total_rows,), jnp.int32).at[order].set(jnp.arange(total_rows, dtype=jnp.int32))
    )
    own_pos = first_row + jnp.arange(rows_here, dtype=jnp.int32)
    own_cols = lax.dynamic_slice_in_dim(dens_cols, first_row, rows_here, 0)
    ham_onehot, dens_pick, pattern = offset_maps(ham_cols, own_cols, own_pos, own_pos, inverse)
    by_offset, cheb_zero, cheb_one = first_terms(ham_onehot, ham_blocks, pattern, block_size)
    fermi = coefficients[0] * cheb_zero + coefficients[1] * cheb_one
    previous, current = (cheb_zero, cheb_one)
    for term in range(2, TERMS):
        rounded = current.astype(jnp.bfloat16)
        lower_rows = from_behind(rounded, "rows", 1)
        upper_rows = from_behind(rounded, "rows", -1)
        window = jnp.concatenate([lower_rows, rounded, upper_rows], axis=0)
        summed = apply_ham(window, rows_here, by_offset, rows_here)
        following = 2.0 * summed * pattern[:, None, :, None] - previous
        fermi = fermi + coefficients[term] * following
        previous, current = (current, following)
    return to_slots(fermi, dens_pick)


def solution(mesh):
    return jax.shard_map(
        local,
        mesh=mesh,
        in_specs=(P(), P("rows", None), P(), P("rows", None, None, None), P()),
        out_specs=P("rows", None, None, None),
        check_vma=False,
    )
```

profile of v0, /device:TPU:6, one launch (start us, length us, event | category | flops | bytes accessed | tf_op | source)
XLA Modules:
  0.0 594.3 jit_solution(8702551376676044798)
XLA Ops:
  4.0 6.4 %scatter_custom_fusion = s32[1152]{0:T(1024)S(1)} fusion(s32[1152]{0:T(1024)S(1)} %compare_select_fusion, s32[1152]{0:T(1024)S(1)} %iota.52, s32[]{:T(128)} %constant.131.clone.1), kind=kCustom, calls=%fused_computation.103 | custom fusion | bytes 4612 | tf_op jit(solution)/shard_map/scatter | solution.py:106
  13.9 5.8 convolution_convert_fusion
  19.7 6.4 %fusion.18 = (bf16[9,128,19,128]{3,2,1,0:T(8,128)(2,1)S(1)}, f32[19,9,128,128]{3,0,2,1:T(8,128)}) fusion(f32[9,19]{1,0:T(8,128)S(1)} %convert_reduce_fusion, bf16[9,9,128,128]{3,1,2,0:T(8,128)(2,1)S(1)} %convolution_convert_fusion, s32[9]{0:T(128)S(1)} %iota_add_fusion.1), kind=kOutput, calls=%fused_computation.64 | convolution fusion | flops 56033452 | bytes 19464912 | tf_op jit(solution)/shard_map/dpxy,de->pxey/dot_general | solution.py:50
  32.6 8.3 %collective-permute-start.1 = (bf16[9,128,19,128]{3,1,2,0:T(8,128)(2,1)}, bf16[9,128,19,128]{3,1,2,0:T(8,128)(2,1)}, u32[]{:S(2)}, u32[]{:S(2)}) collective-permute-start(bf16[9,128,19,128]{3,1,2,0:T(8,128)(2,1)} %copy.34), channel_id=1, source_target_pairs={{1,0},{2,1},{3,2},{4,3},{5,4},{6,5},{7,6},{8,7},{9,8},{10,9},{11,1... | collective-permute-start | bytes 16809992 | tf_op jit(solution)/shard_map/ppermute | solution.py:14
  40.9 6.5 %copy.33 = bf16[9,128,9,128]{1,3,2,0:T(8,128)(2,1)} copy(bf16[9,128,9,128]{3,2,1,0:T(8,128)(2,1)} %bitcast.201) | data formatting | bytes 5308416 | tf_op jit(solution)/shard_map/convert_element_type | solution.py:44
  54.1 46.3 %collective-permute-done = bf16[9,128,19,128]{3,1,2,0:T(8,128)(2,1)} collective-permute-done((bf16[9,128,19,128]{3,1,2,0:T(8,128)(2,1)}, bf16[9,128,19,128]{3,1,2,0:T(8,128)(2,1)}, u32[]{:S(2)}, u32[]{:S(2)}) %collective-permute-start) | collective-permute-done | bytes 5603360 | tf_op jit(solution)/shard_map/ppermute | solution.py:14
  100.4 6.7 %copy.36 = bf16[9,128,19,128]{3,2,1,0:T(8,128)(2,1)S(1)} copy(bf16[9,128,19,128]{3,1,2,0:T(8,128)(2,1)} %collective-permute-done) | data formatting | bytes 11206656 | tf_op jit(solution)/shard_map/ppermute | solution.py:14
  107.1 9.7 %copy.37 = bf16[9,128,19,128]{3,2,1,0:T(8,128)(2,1)} copy(bf16[9,128,19,128]{3,1,2,0:T(8,128)(2,1)} %collective-permute-done.1) | data formatting | bytes 11206656 | tf_op jit(solution)/shard_map/ppermute | solution.py:14
  116.8 13.2 %pad_maximum_fusion = bf16[27,128,19,128]{3,2,1,0:T(8,128)(2,1)} fusion(bf16[9,128,19,128]{3,2,1,0:T(8,128)(2,1)} %copy.37, bf16[9,128,19,128]{3,2,1,0:T(8,128)(2,1)S(1)} %bitcast.180, bf16[9,128,19,128]{3,2,1,0:T(8,128)(2,1)S(1)} %copy.36), kind=kLoop, calls=%fused_computation.49 | loop fusion | flops 16809984 | bytes 33619968 | tf_op jit(solution)/shard_map/concatenate | solution.py:118
  130.0 25.7 %copy.39 = bf16[27,128,19,128]{1,3,2,0:T(8,128)(2,1)} copy(bf16[27,128,19,128]{3,2,1,0:T(8,128)(2,1)} %pad_maximum_fusion) | data formatting | bytes 33619968 | tf_op jit(solution)/shard_map/while | solution.py:87
  155.7 5.5 broadcast.131.clone
  161.2 116.4 %while.28 = (s32[]{:T(128)}, f32[9,128,19,128]{3,1,2,0:T(8,128)}, bf16[9,128,1152]{2,1,0:T(8,128)(2,1)}, s32[9]{0:T(128)S(1)}, bf16[27,128,19,128]{1,3,2,0:T(8,1...) while((s32[]{:T(128)}, f32[9,128,19,128]{3,1,2,0:T(8,128)}, ...), condition=%wide.region_3.4_spmd, body=%wide.region_2.3_spmd.sunk | while | flops 717225984 | bytes 47514992 | solution.py:87
  277.6 17.0 %fusion.19 = bf16[9,128,19,128]{3,2,1,0:T(8,128)(2,1)} fusion(f32[9,128,19,128]{3,1,2,0:T(8,128)} %get-tuple-element.213, f32[9,19]{1,0:T(8,128)S(1)} %broadcast_multiply_fusion.1, f32[9,19]{1,0:T(8,128)S(1)} %convert_reduce_fusion, f32[128,19,128]{2,1,0:T(8,128)} %broadcast_multiply_fusion), kind=kLoop, calls=%fused_computation.65 | loop fusion | flops 11206656 | bytes 18056536 | tf_op jit(solution)/shard_map/convert_element_type | solution.py:115
  294.6 7.1 %copy.41 = bf16[9,128,19,128]{3,1,2,0:T(8,128)(2,1)} copy(bf16[9,128,19,128]{3,2,1,0:T(8,128)(2,1)} %fusion.19) | data formatting | bytes 11206656 | tf_op jit(solution)/shard_map/convert_element_type | solution.py:115
  303.6 8.0 %collective-permute-start.3 = (bf16[9,128,19,128]{3,1,2,0:T(8,128)(2,1)}, bf16[9,128,19,128]{3,1,2,0:T(8,128)(2,1)}, u32[]{:S(2)}, u32[]{:S(2)}) collective-permute-start(bf16[9,128,19,128]{3,1,2,0:T(8,128)(2,1)} %copy.41), channel_id=1, source_target_pairs={{1,0},{2,1},{3,2},{4,3},{5,4},{6,5},{7,6},{8,7},{9,8},{10,9},{11,1... | collective-permute-start | bytes 16809992 | tf_op jit(solution)/shard_map/ppermute | solution.py:14
  312.3 58.8 %collective-permute-done.2 = bf16[9,128,19,128]{3,1,2,0:T(8,128)(2,1)} collective-permute-done((bf16[9,128,19,128]{3,1,2,0:T(8,128)(2,1)}, bf16[9,128,19,128]{3,1,2,0:T(8,128)(2,1)}, u32[]{:S(2)}, u32[]{:S(2)}) %collective-permute-start.2) | collective-permute-done | bytes 5603360 | tf_op jit(solution)/shard_map/ppermute | solution.py:14
  371.1 6.7 %copy.43 = bf16[9,128,19,128]{3,2,1,0:T(8,128)(2,1)S(1)} copy(bf16[9,128,19,128]{3,1,2,0:T(8,128)(2,1)} %collective-permute-done.2) | data formatting | bytes 11206656 | tf_op jit(solution)/shard_map/ppermute | solution.py:14
  377.9 9.7 %copy.44 = bf16[9,128,19,128]{3,2,1,0:T(8,128)(2,1)} copy(bf16[9,128,19,128]{3,1,2,0:T(8,128)(2,1)} %collective-permute-done.3) | data formatting | bytes 11206656 | tf_op jit(solution)/shard_map/ppermute | solution.py:14
  387.6 13.2 %pad_maximum_fusion.1 = bf16[27,128,19,128]{3,2,1,0:T(8,128)(2,1)} fusion(bf16[9,128,19,128]{3,2,1,0:T(8,128)(2,1)} %copy.44, bf16[9,128,19,128]{3,2,1,0:T(8,128)(2,1)S(1)} %bitcast.182, bf16[9,128,19,128]{3,2,1,0:T(8,128)(2,1)S(1)} %copy.43), kind=kLoop, calls=%fused_computation.50 | loop fusion | flops 16809984 | bytes 33619968 | tf_op jit(solution)/shard_map/concatenate | solution.py:118
  400.7 25.7 %copy.46 = bf16[27,128,19,128]{1,3,2,0:T(8,128)(2,1)} copy(bf16[27,128,19,128]{3,2,1,0:T(8,128)(2,1)} %pad_maximum_fusion.1) | data formatting | bytes 33619968 | tf_op jit(solution)/shard_map/while | solution.py:87
  426.5 5.7 broadcast.131
  432.1 115.9 %while.29 = (s32[]{:T(128)}, f32[9,128,19,128]{3,1,2,0:T(8,128)}, bf16[9,128,1152]{2,1,0:T(8,128)(2,1)}, s32[9]{0:T(128)S(1)}, bf16[27,128,19,128]{1,3,2,0:T(8,1...) while((s32[]{:T(128)}, f32[9,128,19,128]{3,1,2,0:T(8,128)}, ...), condition=%wide.region_5.6_spmd, body=%wide.region_4.5_spmd.sunk | while | flops 717225984 | bytes 47514992 | solution.py:87
  548.1 35.4 %fusion.11 = f32[9,16,128,128]{3,1,2,0:T(8,128)} fusion(f32[9,128,19,128]{3,1,2,0:T(8,128)} %get-tuple-element.214, f32[19,9,128,128]{3,0,2,1:T(8,128)} %get-tuple-element.288, f32[9,128,19,128]{3,1,2,0:T(8,128)} %get-tuple-element.213, f32[]{:T(128)} %bitcast.61, f32[9,19]{1,0:T(8,128)S(1)} %broadcast_multiply_fusion.1, f32[]{:T(128)} %bitcast.58, ...), kind=kOutput, calls=%fused_computation.56 | convolution fusion | flops 574346624 | bytes 44304516 | tf_op jit(solution)/shard_map/pae,pxez->paxz/dot_general | solution.py:91
  583.6 10.3 %copy.48 = f32[9,16,128,128]{3,2,1,0:T(8,128)} copy(f32[9,16,128,128]{3,1,2,0:T(8,128)} %fusion.11) | data formatting | bytes 18874368 | tf_op jit(solution)/shard_map/pae,pxez->paxz/dot_general | solution.py:91
  (574 shorter events, 227.8 us)
Async XLA Ops:
  0.0 13.9 %copy-start = (bf16[9,8,128,128]{3,2,1,0:T(8,128)(2,1)S(1)}, bf16[9,8,128,128]{3,2,1,0:T(8,128)(2,1)}, u32[]{:S(2)}) copy-start(bf16[9,8,128,128]{3,2,1,0:T(8,128)(2,1)} %param.12) | copy-start | bytes 7077892
  1.8 12.0 %copy-start.9 = (s32[19]{0:T(128)}, s32[19]{0:T(128)S(1)}, u32[]{:S(2)}) copy-start(s32[19]{0:T(128)S(1)} %iota_add_fusion.2) | copy-start | bytes 232
  12.1 7.6 %copy-start.6 = (pred[9,16]{1,0:T(8,128)(4,1)}, pred[9,16]{1,0:T(8,128)(4,1)S(1)}, u32[]{:S(2)}) copy-start(pred[9,16]{1,0:T(8,128)(4,1)S(1)} %copy.29) | copy-start | bytes 436
  13.6 12.5 %copy-start.4 = (s32[9,16]{1,0:T(8,128)}, s32[9,16]{1,0:T(8,128)S(1)}, u32[]{:S(2)}) copy-start(s32[9,16]{1,0:T(8,128)S(1)} %broadcast_subtract_fusion.1) | copy-start | bytes 1732
  19.7 6.4 %copy-start.3 = (bf16[9,9,128,128]{3,1,2,0:T(8,128)(2,1)}, bf16[9,9,128,128]{3,1,2,0:T(8,128)(2,1)S(1)}, u32[]{:S(2)}) copy-start(bf16[9,9,128,128]{3,1,2,0:T(8,128)(2,1)S(1)} %convolution_convert_fusion) | copy-start | bytes 7962628
  26.1 4.6 copy-start.2
  30.7 69.7 %collective-permute-start = (bf16[9,128,19,128]{3,1,2,0:T(8,128)(2,1)}, bf16[9,128,19,128]{3,1,2,0:T(8,128)(2,1)}, u32[]{:S(2)}, u32[]{:S(2)}) collective-permute-start(bf16[9,128,19,128]{3,1,2,0:T(8,128)(2,1)} %copy.34), channel_id=1, source_target_pairs={{0,1},{1,2},{2,3},{3,4},{4,5},{5,6},{6,7},{7,8},{8,9},{9,10},{10,1... | collective-permute-start | bytes 16809992 | tf_op jit(solution)/shard_map/ppermute | solution.py:14
  32.6 74.5 %collective-permute-start.1 = (bf16[9,128,19,128]{3,1,2,0:T(8,128)(2,1)}, bf16[9,128,19,128]{3,1,2,0:T(8,128)(2,1)}, u32[]{:S(2)}, u32[]{:S(2)}) collective-permute-start(bf16[9,128,19,128]{3,1,2,0:T(8,128)(2,1)} %copy.34), channel_id=1, source_target_pairs={{1,0},{2,1},{3,2},{4,3},{5,4},{6,5},{7,6},{8,7},{9,8},{10,9},{11,1... | collective-permute-start | bytes 16809992 | tf_op jit(solution)/shard_map/ppermute | solution.py:14
  100.3 16.5 %slice-start = ((s8[7077888]{0:T(1024)(128)(4,1)}), s8[4194304]{0:T(1024)(128)(4,1)S(1)}, s32[]{:S(2)}) async-start(s8[7077888]{0:T(1024)(128)(4,1)} %bitcast.179), calls=%async_computation | async-start | bytes 8388608
  107.1 9.7 %slice-start.1 = ((s8[7077888]{0:T(1024)(128)(4,1)}), s8[2883584]{0:T(1024)(128)(4,1)S(1)}, s32[]{:S(2)}) async-start(s8[7077888]{0:T(1024)(128)(4,1)} %bitcast.179), calls=%async_computation.1 | async-start | bytes 5767168
  294.6 17.1 %copy-start.8 = (f32[4]{0:T(128)S(1)}, f32[4]{0:T(128)}, u32[]{:S(2)}) copy-start(f32[4]{0:T(128)} %param.13) | copy-start | bytes 52
  301.7 69.4 %collective-permute-start.2 = (bf16[9,128,19,128]{3,1,2,0:T(8,128)(2,1)}, bf16[9,128,19,128]{3,1,2,0:T(8,128)(2,1)}, u32[]{:S(2)}, u32[]{:S(2)}) collective-permute-start(bf16[9,128,19,128]{3,1,2,0:T(8,128)(2,1)} %copy.41), channel_id=1, source_target_pairs={{0,1},{1,2},{2,3},{3,4},{4,5},{5,6},{6,7},{7,8},{8,9},{9,10},{10,1... | collective-permute-start | bytes 16809992 | tf_op jit(solution)/shard_map/ppermute | solution.py:14
  303.6 74.3 %collective-permute-start.3 = (bf16[9,128,19,128]{3,1,2,0:T(8,128)(2,1)}, bf16[9,128,19,128]{3,1,2,0:T(8,128)(2,1)}, u32[]{:S(2)}, u32[]{:S(2)}) collective-permute-start(bf16[9,128,19,128]{3,1,2,0:T(8,128)(2,1)} %copy.41), channel_id=1, source_target_pairs={{1,0},{2,1},{3,2},{4,3},{5,4},{6,5},{7,6},{8,7},{9,8},{10,9},{11,1... | collective-permute-start | bytes 16809992 | tf_op jit(solution)/shard_map/ppermute | solution.py:14
  371.1 16.4 %slice-start.2 = ((s8[7077888]{0:T(1024)(128)(4,1)}), s8[4194304]{0:T(1024)(128)(4,1)S(1)}, s32[]{:S(2)}) async-start(s8[7077888]{0:T(1024)(128)(4,1)} %bitcast.181), calls=%async_computation.2 | async-start | bytes 8388608
  377.9 9.7 %slice-start.3 = ((s8[7077888]{0:T(1024)(128)(4,1)}), s8[2883584]{0:T(1024)(128)(4,1)S(1)}, s32[]{:S(2)}) async-start(s8[7077888]{0:T(1024)(128)(4,1)} %bitcast.181), calls=%async_computation.3 | async-start | bytes 5767168
  432.1 116.0 %copy-start.5 = (s32[9,16]{1,0:T(8,128)S(1)}, s32[9,16]{1,0:T(8,128)}, u32[]{:S(2)}) copy-start(s32[9,16]{1,0:T(8,128)} %copy-done.4) | copy-start | bytes 1732
  432.1 116.0 %copy-start.7 = (pred[9,16]{1,0:T(8,128)(4,1)S(1)}, pred[9,16]{1,0:T(8,128)(4,1)}, u32[]{:S(2)}) copy-start(pred[9,16]{1,0:T(8,128)(4,1)} %copy-done.6) | copy-start | bytes 436
  432.1 116.0 %copy-start.10 = (s32[19]{0:T(128)S(1)}, s32[19]{0:T(128)}, u32[]{:S(2)}) copy-start(s32[19]{0:T(128)} %copy-done.9) | copy-start | bytes 232
  548.1 45.7 %copy-start.1 = (bf16[9,8,128,128]{3,2,1,0:T(8,128)(2,1)S(1)}, bf16[9,8,128,128]{3,2,1,0:T(8,128)(2,1)}, u32[]{:S(2)}) copy-start(bf16[9,8,128,128]{3,2,1,0:T(8,128)(2,1)} %param.12) | copy-start | bytes 7077892
where the time goes:
time: 603 us; the launch traced here: 594 us
  local copies, waits for them, and re-layouts  276 us (46%)
  matrix products  116 us (19%)
  waiting for transfers between devices  105 us (17%)
  other arithmetic  48.9 us (8%)
  loops' own time  27.7 us (5%)
  starting transfers between devices  20.2 us (3%)
    ppermute x4, waiting for transfers between devices, from_behind(): return lax.ppermute(block, axis, route)  105 us
    squeeze x18, local copies, waits for them, and re-layouts, one_row(): piece = nearby[slot]  88.1 us
    dot_general x18, matrix products, one_row(): jnp.dot(row_left, stacked, preferred_element_type=jnp.float32)  67.9 us
    while x3, local copies, waits for them, and re-layouts, apply_ham(): return lax.map(one_row, (left_rows, jnp.arange(count, dtype=jnp.int32)))  56.7 us
    dot_general x1, matrix products, to_slots(): jnp.einsum('pae,pxez->paxz', dens_pick, fermi, precision=lax.Precision.HI...  35.4 us
    ppermute x4, local copies, waits for them, and re-layouts, from_behind(): return lax.ppermute(block, axis, route)  32.9 us
    another operation x2, loops' own time, apply_ham(): return lax.map(one_row, (left_rows, jnp.arange(count, dtype=jnp.int32)))  27.7 us
    concatenate x2, other arithmetic, local(): window = jnp.concatenate([lower_rows, rounded, upper_rows], axis=0)  26.3 us
  transfers between devices with their start and end apart: 4, of which 2 were waited for; matrix products, arithmetic and copies ran while one was open for 5% of the time, Pallas kernels for 0%

commit v1 on v0

v1 whole, which is shorter than its diff:
```python
import functools

import jax
import jax.numpy as jnp
from jax import lax
from jax.experimental import pallas as pl
from jax.experimental.pallas import tpu as pltpu
from jax.sharding import PartitionSpec as P

REACH = 4
PREACH = 9
BS = 128
KH = 8
KP = 16
OWN = 9
HALO = 2 * REACH
CHUNKS = (5, 2, 1)

H_ROWS = OWN + 2 * HALO
T_ROWS = OWN + 2 * REACH
COLS = 40
NO_COL = 35
FIRST_COL = REACH + PREACH
H_ZERO = H_ROWS * KH
T_ZERO = T_ROWS * KP
META = 5

VMEM = pl.BlockSpec(memory_space=pltpu.VMEM)
SMEM = pl.BlockSpec(memory_space=pltpu.SMEM)
ANY = pl.BlockSpec(memory_space=pl.ANY)


def as_blocks(ref):
    if len(ref.shape) == 3:
        return ref
    rows = ref.shape[0] // BS
    return ref.at[pl.ds(0, rows * BS)].reshape(rows, BS, BS)


def stage(copies, terms, finals, first, *refs):
    n = len(copies)
    odd_ref, coef, h_index, t_index, d_col, h_base, t_base = refs[:7]
    arrived = refs[7 : 7 + n]
    ham, cheb, part, out, sems = refs[-5:]
    odd = odd_ref[0]
    eye = (
        lax.broadcasted_iota(jnp.int32, (BS, BS), 0) == lax.broadcasted_iota(jnp.int32, (BS, BS), 1)
    ).astype(jnp.float32)
    c0, c1, c2, c3 = coef[0], coef[1], coef[2], coef[3]

    moves = []
    for i, (rows, source, even_at, odd_at) in enumerate(copies):
        blocks = rows * KH
        start = 0 if source is None else jnp.where(odd == 1, source[1], source[0]) * KH
        at = jnp.where(odd == 1, odd_at, even_at) * KH
        move = pltpu.make_async_copy(
            as_blocks(arrived[i]).at[pl.ds(start, blocks)], ham.at[pl.ds(at, blocks)], sems.at[i]
        )
        move.start()
        moves.append(move)
    if first:
        ham[H_ZERO] = jnp.zeros((BS, BS), jnp.bfloat16)
        cheb[T_ZERO] = jnp.zeros((BS, BS), jnp.bfloat16)
    for move in moves:
        move.wait()

    def row_of(low, t):
        return jnp.where(odd == 1, low + HALO + OWN - 1 + t, HALO - low - t)

    def term_row(w, own):
        j = w - REACH
        r = w - HALO
        left = jnp.concatenate([ham[w * KH + b] for b in range(KH)], axis=1)
        bases = [h_base[w * KH + b] for b in range(KH)]
        for group in range(KP // 4):
            cols = [d_col[j * KP + group * 4 + t] for t in range(4)]
            right = jnp.concatenate(
                [jnp.concatenate([ham[h_index[base + q]] for q in cols], axis=1) for base in bases],
                axis=0,
            )
            total = jnp.dot(left, right, preferred_element_type=jnp.float32)
            for t in range(4):
                q = cols[t]
                on_diagonal = (q == w + (FIRST_COL - HALO)).astype(jnp.float32)
                value = 2.0 * total[:, t * BS : (t + 1) * BS] - on_diagonal * eye
                cheb[j * KP + group * 4 + t] = value.astype(jnp.bfloat16)
                if own:
                    one = ham[h_index[w * COLS + q]].astype(jnp.float32)
                    part[r * KP + group * 4 + t] = (
                        c2 * value + (c1 - c3) * one + (c0 * on_diagonal) * eye
                    )

    def final_row(w):
        r = w - HALO
        left = jnp.concatenate([ham[w * KH + b] for b in range(KH)], axis=1)
        bases = [t_base[r * KH + b] for b in range(KH)]
        for group in range(KP // 4):
            cols = [d_col[(w - REACH) * KP + group * 4 + t] for t in range(4)]
            right = jnp.concatenate(
                [jnp.concatenate([cheb[t_index[base + q]] for q in cols], axis=1) for base in bases],
                axis=0,
            )
            total = jnp.dot(left, right, preferred_element_type=jnp.float32)
            for t in range(4):
                at = r * KP + group * 4 + t
                part[at] = part[at] + (2.0 * c3) * total[:, t * BS : (t + 1) * BS]

    def send_row(t):
        r = row_of(finals[0], t) - HALO
        return pltpu.make_async_copy(
            part.at[pl.ds(r * KP, KP)], out.at[pl.ds(r * KP, KP)], sems.at[n + t]
        )

    for low, high, own in terms:

        def make(t, _, low=low, own=own):
            term_row(row_of(low, t), own)
            return 0

        lax.fori_loop(0, high - low, make, 0)

    def finish(t, _):
        final_row(row_of(finals[0], t))
        send_row(t).start()
        return 0

    def wait(t, _):
        send_row(t).wait()
        return 0

    lax.fori_loop(0, finals[1] - finals[0], finish, 0)
    lax.fori_loop(0, finals[1] - finals[0], wait, 0)


def run_stage(copies, terms, finals, scalars, arrived, state):
    shapes = (
        pltpu.VMEM((H_ZERO + 1, BS, BS), jnp.bfloat16),
        pltpu.VMEM((T_ZERO + 1, BS, BS), jnp.bfloat16),
        pltpu.VMEM((OWN * KP, BS, BS), jnp.float32),
        jax.ShapeDtypeStruct((OWN * KP, BS, BS), jnp.float32),
    )
    n = len(arrived)
    extra = [] if state is None else list(state)
    rows = sum(high - low for low, high, _ in terms) + finals[1] - finals[0]
    return pl.pallas_call(
        functools.partial(stage, copies, terms, finals, state is None),
        out_shape=shapes,
        in_specs=[SMEM] * 7 + [ANY] * n + [VMEM, VMEM, VMEM, ANY][: len(extra)],
        out_specs=(VMEM, VMEM, VMEM, ANY),
        scratch_shapes=[pltpu.SemaphoreType.DMA((n + finals[1] - finals[0],))],
        input_output_aliases={7 + n + i: i for i in range(len(extra))},
        cost_estimate=pl.CostEstimate(
            flops=rows * KH * KP * 2 * BS**3, bytes_accessed=rows * KH * BS * BS * 2, transcendentals=0
        ),
        compiler_params=pltpu.CompilerParams(vmem_limit_bytes=8 << 20),
    )(*scalars, *arrived, *extra)


def columns_of(ids, order_window):
    found = ids[:, :, None] == order_window[None, None, :]
    places = jnp.arange(order_window.shape[0], dtype=jnp.int32) - NO_COL
    return jnp.sum(jnp.where(found, places[None, None, :], 0), axis=2) + NO_COL


def index_of(cols, spare, kept=None):
    rows, slots = cols.shape
    number = jnp.arange(rows * slots, dtype=jnp.int32).reshape(rows, slots, 1) - spare
    wanted = jnp.arange(COLS, dtype=jnp.int32)[None, None, :]
    hit = (cols[:, :, None] == wanted) & (wanted != NO_COL)
    if kept is not None:
        hit = hit & kept[:, None, :]
    table = jnp.sum(jnp.where(hit, number, 0), axis=1) + spare
    return jnp.pad(table, ((0, 1), (0, 0)), constant_values=spare).reshape(-1)


def base_of(cols, first, rows):
    return (jnp.where(cols == NO_COL, rows, cols - first) * COLS).reshape(-1)


def local(order, ham_cols, dens_cols, ham_blocks, coefficients):
    axis = "rows"
    size = lax.axis_size(axis)
    me = lax.axis_index(axis)
    odd = me & 1
    first_row = me * OWN
    near_pairs = [(i, i ^ 1) for i in range(size)]
    far_pairs = [(i, i + 1 if i % 2 else i - 1) for i in range(1, size - 1)]

    order_window = lax.dynamic_slice_in_dim(
        jnp.pad(order, (FIRST_COL, FIRST_COL), constant_values=-2), first_row, OWN + 2 * FIRST_COL, 0
    )
    dens_window = lax.dynamic_slice_in_dim(
        jnp.pad(dens_cols, ((HALO, HALO), (0, 0)), constant_values=-1), first_row, H_ROWS, 0
    )
    own_rows = jnp.arange(OWN, dtype=jnp.int32)[:, None]
    own_cols = columns_of(ham_cols, order_window)
    own_step = jnp.where(own_cols == NO_COL, 0, own_cols - (own_rows + (FIRST_COL - META)))
    all_cols = columns_of(dens_window, order_window)
    d_cols = all_cols[REACH : REACH + T_ROWS]

    blocks = ham_blocks.reshape(OWN * KH, BS, BS)
    far, k = [], 1
    for i, rows in enumerate(CHUNKS):
        start = jnp.where(odd == 1, OWN + 1 - k - rows, k - 1)
        piece = lax.dynamic_slice_in_dim(blocks, start * KH, rows * KH, 0).reshape(rows * KH * BS, BS)
        if i == 0:
            steps = lax.dynamic_slice_in_dim(own_step, jnp.where(odd == 1, 1, 0), HALO, 0)
            steps = jnp.pad(steps.astype(jnp.bfloat16), ((0, 16 - HALO), (0, BS - KH)))
            piece = jnp.concatenate([piece, steps], axis=0)
        far.append(lax.ppermute(piece, axis, far_pairs))
        k += rows
    near_blocks = lax.ppermute(blocks, axis, near_pairs)
    near_step = lax.ppermute(own_step, axis, near_pairs)

    def window_cols(far_step):
        near_rows = jnp.where(odd == 1, near_step[1:], near_step[:HALO])
        before = jnp.where(odd == 1, near_rows, far_step)
        after = jnp.where(odd == 1, far_step, near_rows)
        steps = jnp.concatenate([before, own_step, after], axis=0)
        rows = jnp.arange(H_ROWS, dtype=jnp.int32)[:, None] + (FIRST_COL - HALO - META)
        return jnp.where(steps == 0, NO_COL, steps + rows)

    odd_scalar = odd.astype(jnp.int32).reshape(1)
    t_index = index_of(d_cols, T_ZERO)
    t_base = base_of(own_cols, FIRST_COL - REACH, T_ROWS)

    wanted = jnp.arange(COLS, dtype=jnp.int32)[None, None, :]
    kept = jnp.any(all_cols[:, :, None] == wanted, axis=1)

    def scalars(far_step):
        h_cols = window_cols(far_step)
        return (
            odd_scalar,
            coefficients,
            index_of(h_cols, H_ZERO, kept),
            t_index,
            d_cols.reshape(-1),
            base_of(h_cols, FIRST_COL - HALO, H_ROWS),
            t_base,
        )

    early = scalars(jnp.zeros((HALO, KH), jnp.int32))
    state = run_stage(
        ((OWN, None, HALO, HALO), (HALO, (0, 1), HALO + OWN, 0)),
        ((-3 * REACH, -HALO, False), (-HALO, -REACH + 1, True)),
        (-HALO, -HALO + 1),
        early,
        (blocks, near_blocks),
        None,
    )
    late, k = None, 1
    for rows, piece in zip(CHUNKS, far):
        if late is None:
            steps = piece[rows * KH * BS : rows * KH * BS + HALO, :KH]
            late = scalars(steps.astype(jnp.int32))
        last = k + rows - 1
        low, high = k - REACH, last - REACH + 1
        terms = []
        if low < 1:
            terms.append((low, min(high, 1), True))
        if high > 1:
            terms.append((max(low, 1), high, False))
        state = run_stage(
            ((rows, None, HALO - last, HALO + OWN - 1 + k),),
            tuple(terms),
            (k - HALO, last - HALO + 1),
            late,
            (piece.reshape(-1, BS, BS) if piece.shape[0] % BS == 0 else piece,),
            state,
        )
        k += rows
    return state[3].reshape(OWN, KP, BS, BS)


def solution(mesh):
    return jax.shard_map(
        local,
        mesh=mesh,
        in_specs=(P(), P("rows", None), P(), P("rows", None, None, None), P()),
        out_specs=P("rows", None, None, None),
        check_vma=False,
    )
```

time: 603 us -> 61.8 us (0.10); the launches traced: 594 us -> 61.5 us
  local copies, waits for them, and re-layouts: 276 us -> 4.72 us
  matrix products: 116 us -> 0 us
  waiting for transfers between devices: 105 us -> 3.47 us
  other arithmetic: 48.9 us -> 4.88 us
  Pallas kernels: 0 us -> 29.5 us
  loops' own time: 27.7 us -> 0 us
    dot_general x21 -> x0, matrix products: 116 us -> none  [the longest x18 67.9 us: one_row(): jnp.dot(row_left, stacked, preferred_element_type=jnp.float32)]
    ppermute x4 -> x5, waiting for transfers between devices: 105 us -> 3.47 us  [the longest x3 3.47 us: local(): far.append(lax.ppermute(piece, axis, far_pairs))]
    squeeze x18 -> x0, local copies, waits for them, and re-layouts: 88.1 us -> none  [one_row(): piece = nearby[slot]]
    while x147 -> x0, local copies, waits for them, and re-layouts: 77.4 us -> none  [the longest x3 56.7 us: apply_ham(): return lax.map(one_row, (left_rows, jnp.arange(count, dtype=jnp.int32)))]
    ppermute x4 -> x0, local copies, waits for them, and re-layouts: 32.9 us -> none  [from_behind(): return lax.ppermute(block, axis, route)]
    pallas_call x0 -> x4, Pallas kernels: none -> 29.5 us  [run_stage(): pl.pallas_call(functools.partial(stage, copies, terms, finals, state is N...]
    another operation x2 -> x0, loops' own time: 27.7 us -> none  [apply_ham(): return lax.map(one_row, (left_rows, jnp.arange(count, dtype=jnp.int32)))]
    concatenate x2 -> x1, other arithmetic: 26.3 us -> 1.14 us  [local(): piece = jnp.concatenate([piece, steps], axis=0)]
  transfers between devices with their start and end apart: 4 -> 5, of which waited for: 2 -> 1; matrix products, arithmetic and copies ran while one was open for 5% -> 12% of each run, Pallas kernels for 0% -> 43%
where the time goes in v1:
time: 61.8 us; the launch traced here: 61.5 us
  Pallas kernels  29.5 us (48%)
  starting transfers between devices  18.6 us (30%)
  other arithmetic  4.88 us (8%)
  local copies, waits for them, and re-layouts  4.72 us (8%)
  waiting for transfers between devices  3.47 us (6%)
    pallas_call x4, Pallas kernels, run_stage(): pl.pallas_call(functools.partial(stage, copies, terms, finals, state is N...  29.5 us
    ppermute x3, starting transfers between devices, local(): far.append(lax.ppermute(piece, axis, far_pairs))  18.1 us
    ppermute x3, waiting for transfers between devices, local(): far.append(lax.ppermute(piece, axis, far_pairs))  3.47 us
    dynamic_slice x3, local copies, waits for them, and re-layouts, local(): lax.dynamic_slice_in_dim(blocks, start * KH, rows * KH, 0)  2.47 us
  transfers between devices with their start and end apart: 5, of which 1 were waited for; matrix products, arithmetic and copies ran while one was open for 12% of the time, Pallas kernels for 43%

profile of v1, /device:TPU:6, one launch (start us, length us, event | category | flops | bytes accessed | tf_op | source)
XLA Modules:
  0.0 61.5 jit_solution(13755833985294272675)
XLA Ops:
  0.0 0.8 %copy.34 = s32[9,8]{1,0:T(8,128)S(1)} copy(s32[9,8]{0,1:T(8,128)} %param.6) | data formatting | bytes 576 | tf_op args[1]
  0.8 0.8 %pad_dynamic-slice_fusion.1 = (s32[35]{0:T(128)S(1)}, s32[35]{0:T(128)S(1)}) fusion(s32[]{:T(128)S(6)} %select_n.122, s32[1152]{0:T(1024)} %param.5), kind=kLoop, calls=%fused_computation.26 | loop fusion | flops 35 | bytes 4892 | tf_op jit(solution)/shard_map/dynamic_slice | solution.py:189
  1.5 0.3 select_reduce_fusion.4
  2.0 0.5 collective-permute-start.4
  2.5 1.6 %constant_dynamic-slice_fusion.2 = bf16[40,128,128]{2,1,0:T(8,128)(2,1)S(1)} fusion(bf16[72,128,128]{2,1,0:T(8,128)(2,1)} %bitcast.9, s32[]{:T(128)S(6)} %select_n.127), kind=kLoop, calls=%fused_computation.43 | loop fusion | bytes 2621444 | tf_op jit(solution)/shard_map/dynamic_slice | solution.py:205
  4.1 1.1 %fusion.1 = bf16[5136,128]{1,0:T(8,128)(2,1)} fusion(bf16[8,8]{1,0:T(8,128)(2,1)S(1)} %dynamic-slice_convert_fusion, bf16[5120,128]{1,0:T(8,128)(2,1)S(1)} %bitcast.15), kind=kLoop, calls=%fused_computation.2 | loop fusion | flops 3944448 | bytes 2625664 | tf_op jit(solution)/shard_map/concatenate | solution.py:209
  5.3 8.3 %collective-permute-start.1 = (bf16[5136,128]{1,0:T(8,128)(2,1)}, bf16[5136,128]{1,0:T(8,128)(2,1)}, u32[]{:S(2)}, u32[]{:S(2)}) collective-permute-start(bf16[5136,128]{1,0:T(8,128)(2,1)} %fusion.1), channel_id=1, source_target_pairs={{1,2},{2,1},{3,4},{4,3},{5,6},{6,5},{7,8},{8,7},{9,10},{10,9},{11,... | collective-permute-start | bytes 3944456 | tf_op jit(solution)/shard_map/ppermute | solution.py:210
  13.6 0.8 %constant_dynamic-slice_fusion = bf16[16,128,128]{2,1,0:T(8,128)(2,1)} fusion(bf16[72,128,128]{2,1,0:T(8,128)(2,1)S(1)} %bitcast.10, s32[]{:T(128)S(6)} %select_n.142), kind=kLoop, calls=%fused_computation.41 | loop fusion | bytes 1048580 | tf_op jit(solution)/shard_map/dynamic_slice | solution.py:205
  14.5 1.9 %collective-permute-start.3 = (bf16[2048,128]{1,0:T(8,128)(2,1)}, bf16[2048,128]{1,0:T(8,128)(2,1)S(1)}, u32[]{:S(2)}, u32[]{:S(2)}) collective-permute-start(bf16[2048,128]{1,0:T(8,128)(2,1)} %bitcast.5), channel_id=1, source_target_pairs={{1,2},{2,1},{3,4},{4,3},{5,6},{6,5},{7,8},{8,7},{9,10},{10,9},{11,... | collective-permute-start | bytes 1572872 | tf_op jit(solution)/shard_map/ppermute | solution.py:210
  16.4 7.9 %collective-permute-start.2 = (bf16[1024,128]{1,0:T(8,128)(2,1)S(1)}, bf16[1024,128]{1,0:T(8,128)(2,1)S(1)}, u32[]{:S(2)}, u32[]{:S(2)}) collective-permute-start(bf16[1024,128]{1,0:T(8,128)(2,1)S(1)} %bitcast.16), channel_id=1, source_target_pairs={{1,2},{2,1},{3,4},{4,3},{5,6},{6,5},{7,8},{8,7},{9,10},{10,9},{11,... | collective-permute-start | bytes 786440 | tf_op jit(solution)/shard_map/ppermute | solution.py:210
  24.5 0.1 copy.39
  24.5 0.6 select_reduce_fusion
  25.3 0.1 fusion.2
  25.4 0.1 select_reduce_fusion.1
  25.8 3.5 %collective-permute-done.1.refs_7_ = bf16[5136,128]{1,0:T(8,128)(2,1)} collective-permute-done((bf16[5136,128]{1,0:T(8,128)(2,1)}, bf16[5136,128]{1,0:T(8,128)(2,1)}, u32[]{:S(2)}, u32[]{:S(2)}) %collective-permute-start.1) | collective-permute-done | bytes 1314848 | tf_op jit(solution)/shard_map/ppermute | solution.py:210
  29.3 0.7 %convert_select_fusion.1 = (s32[8,8]{1,0:T(8,128)S(1)}, s32[8,8]{1,0:T(8,128)S(1)}) fusion(pred[]{:T(512)S(6)} %eq.129, bf16[5136,128]{1,0:T(8,128)(2,1)} %collective-permute-done.1.refs_7_, s32[9,8]{1,0:T(8,128)S(1)} %collective-permute-done), kind=kLoop, calls=%fused_computation.30 | loop fusion | flops 192 | bytes 1153 | tf_op jit(solution)/shard_map/jit(_where)/select_n | solution.py:217
  29.9 0.7 %convert_select_fusion = (s32[8,8]{1,0:T(8,128)S(1)}, s32[8,8]{1,0:T(8,128)S(1)}, s32[8,8]{1,0:T(8,128)S(1)}) fusion(s32[8,8]{1,0:T(8,128)S(1)} %get-tuple-element.38, pred[]{:T(512)S(6)} %eq.129, bf16[5136,128]{1,0:T(8,128)(2,1)} %collective-permute-done.1.refs_7_), kind=kLoop, calls=%fused_computation.29 | loop fusion | flops 256 | bytes 1153 | tf_op jit(solution)/shard_map/jit(_where)/select_n | solution.py:218
  31.0 0.1 copy.38
  31.2 0.2 select_reduce_fusion.2
  31.7 0.1 copy.40
  31.9 11.0 %shard_map.55 = (bf16[201,128,128]{2,1,0:T(8,128)(2,1)S(1)}, bf16[273,128,128]{2,1,0:T(8,128)(2,1)S(1)}, f32[144,128,128]{2,1,0:T(8,128)S(1)}, f32[144,128,128]{2,1,0:T(8,128)}) custom-call(s32[1]{0:T(128)} %bitcast.refs_0_, f32[4]{0:T(128)S(1)} %copy-done.1, s32[1040]{0:T(1024)S(1)} %reshape.264.refs_2_, s32[720]{0:T(1024)S(1)} %reshape.258.refs_3_, ...), custom_call_target="tpu_custom_call" | custom-call | flops 5368709120 | bytes 2621440 | tf_op jit(solution)/shard_map/pallas_call | solution.py:145
  43.0 10.6 %shard_map.56 = (bf16[201,128,128]{2,1,0:T(8,128)(2,1)S(1)}, bf16[273,128,128]{2,1,0:T(8,128)(2,1)S(1)}, f32[144,128,128]{2,1,0:T(8,128)S(1)}, f32[144,128,128]{2,1,0:T(8,128)}) custom-call(s32[1]{0:T(128)} %bitcast.refs_0_, f32[4]{0:T(128)S(1)} %copy-done.1, ...), custom_call_target="tpu_custom_call", output_to_operand_aliasing={{0}: (8, {}), {1}: (9, {}), {2}: (10, {}), {3}: (11, {})} | custom-call | flops 5368709120 | bytes 2621440 | tf_op jit(solution)/shard_map/pallas_call | solution.py:145
  53.6 4.7 %shard_map.57 = (bf16[201,128,128]{2,1,0:T(8,128)(2,1)S(1)}, bf16[273,128,128]{2,1,0:T(8,128)(2,1)S(1)}, f32[144,128,128]{2,1,0:T(8,128)S(1)}, f32[144,128,128]{2,1,0:T(8,128)}) custom-call(s32[1]{0:T(128)} %bitcast.refs_0_, f32[4]{0:T(128)S(1)} %copy-done.1, ...), custom_call_target="tpu_custom_call", output_to_operand_aliasing={{0}: (8, {}), {1}: (9, {}), {2}: (10, {}), {3}: (11, {})} | custom-call | flops 2147483648 | bytes 1048576 | tf_op jit(solution)/shard_map/pallas_call | solution.py:145
  58.3 3.2 %shard_map.58 = (bf16[201,128,128]{2,1,0:T(8,128)(2,1)S(1)}, bf16[273,128,128]{2,1,0:T(8,128)(2,1)S(1)}, f32[144,128,128]{2,1,0:T(8,128)S(1)}, f32[144,128,128]{2,1,0:T(8,128)}) custom-call(s32[1]{0:T(128)} %bitcast.refs_0_, f32[4]{0:T(128)S(1)} %copy-done.1, ...), custom_call_target="tpu_custom_call", output_to_operand_aliasing={{0}: (8, {}), {1}: (9, {}), {2}: (10, {}), {3}: (11, {})} | custom-call | flops 1073741824 | bytes 524288 | tf_op jit(solution)/shard_map/pallas_call | solution.py:145
  (42 shorter events, 1.5 us)
Async XLA Ops:
  1.9 23.9 %collective-permute-start = (s32[9,8]{1,0:T(8,128)S(1)}, s32[9,8]{1,0:T(8,128)S(1)}, u32[]{:S(2)}, u32[]{:S(2)}) collective-permute-start(s32[9,8]{1,0:T(8,128)S(1)} %get-tuple-element.40), channel_id=1, source_target_pairs={{0,1},{1,0},{2,3},{3,2},{4,5},{5,4},{6,7},{7,6},{8,9},{9,8},{10,11... | collective-permute-start | bytes 872 | tf_op jit(solution)/shard_map/ppermute | solution.py:213
  2.0 30.0 %collective-permute-start.4 = (bf16[72,128,128]{2,1,0:T(8,128)(2,1)}, bf16[72,128,128]{2,1,0:T(8,128)(2,1)}, u32[]{:S(2)}, u32[]{:S(2)}) collective-permute-start(bf16[72,128,128]{2,1,0:T(8,128)(2,1)} %bitcast.8), channel_id=1, source_target_pairs={{0,1},{1,0},{2,3},{3,2},{4,5},{5,4},{6,7},{7,6},{8,9},{9,8},{10,11... | collective-permute-start | bytes 7077896 | tf_op jit(solution)/shard_map/ppermute | solution.py:212
  2.5 11.1 %copy-start = (bf16[9,8,128,128]{3,2,1,0:T(8,128)(2,1)S(1)}, bf16[9,8,128,128]{3,2,1,0:T(8,128)(2,1)}, u32[]{:S(2)}) copy-start(bf16[9,8,128,128]{3,2,1,0:T(8,128)(2,1)} %param.8) | copy-start | bytes 7077892
  4.1 20.3 %copy-start.2 = (s32[1152,16]{0,1:T(8,128)S(1)}, s32[1152,16]{0,1:T(8,128)}, u32[]{:S(2)}) copy-start(s32[1152,16]{0,1:T(8,128)} %param.7) | copy-start | bytes 221188
  4.1 27.8 %copy-start.1 = (f32[4]{0:T(128)S(1)}, f32[4]{0:T(128)}, u32[]{:S(2)}) copy-start(f32[4]{0:T(128)} %refs_1_.7) | copy-start | bytes 52
  5.3 24.0 %collective-permute-start.1 = (bf16[5136,128]{1,0:T(8,128)(2,1)}, bf16[5136,128]{1,0:T(8,128)(2,1)}, u32[]{:S(2)}, u32[]{:S(2)}) collective-permute-start(bf16[5136,128]{1,0:T(8,128)(2,1)} %fusion.1), channel_id=1, source_target_pairs={{1,2},{2,1},{3,4},{4,3},{5,6},{6,5},{7,8},{8,7},{9,10},{10,9},{11,... | collective-permute-start | bytes 3944456 | tf_op jit(solution)/shard_map/ppermute | solution.py:210
  14.5 39.1 %collective-permute-start.3 = (bf16[2048,128]{1,0:T(8,128)(2,1)}, bf16[2048,128]{1,0:T(8,128)(2,1)S(1)}, u32[]{:S(2)}, u32[]{:S(2)}) collective-permute-start(bf16[2048,128]{1,0:T(8,128)(2,1)} %bitcast.5), channel_id=1, source_target_pairs={{1,2},{2,1},{3,4},{4,3},{5,6},{6,5},{7,8},{8,7},{9,10},{10,9},{11,... | collective-permute-start | bytes 1572872 | tf_op jit(solution)/shard_map/ppermute | solution.py:210
  16.4 41.9 %collective-permute-start.2 = (bf16[1024,128]{1,0:T(8,128)(2,1)S(1)}, bf16[1024,128]{1,0:T(8,128)(2,1)S(1)}, u32[]{:S(2)}, u32[]{:S(2)}) collective-permute-start(bf16[1024,128]{1,0:T(8,128)(2,1)S(1)} %bitcast.16), channel_id=1, source_target_pairs={{1,2},{2,1},{3,4},{4,3},{5,6},{6,5},{7,8},{8,7},{9,10},{10,9},{11,... | collective-permute-start | bytes 786440 | tf_op jit(solution)/shard_map/ppermute | solution.py:210

commit v2 on v1

v2 whole, which is shorter than its diff:
```python
import functools

import jax
import jax.numpy as jnp
from jax import lax
from jax.experimental import pallas as pl
from jax.experimental.pallas import tpu as pltpu
from jax.sharding import PartitionSpec as P

REACH = 4
PREACH = 9
BS = 128
KH = 8
KP = 16
OWN = 9
HALO = 2 * REACH
FIRST, SECOND = 5, 3

H_ROWS = OWN + 2 * HALO
T_ROWS = OWN + 2 * REACH
COLS = 40
NO_COL = 35
FIRST_COL = REACH + PREACH
H_ZERO = H_ROWS * KH
T_ZERO = T_ROWS * KP
META = 5
LINE = BS
T_LINES = H_ROWS + 1
LINES = T_LINES + T_ROWS + 1

VMEM = pl.BlockSpec(memory_space=pltpu.VMEM)
SMEM = pl.BlockSpec(memory_space=pltpu.SMEM)
ANY = pl.BlockSpec(memory_space=pl.ANY)


def as_blocks(ref):
    if len(ref.shape) == 3:
        return ref
    rows = ref.shape[0] // BS
    return ref.at[pl.ds(0, rows * BS)].reshape(rows, BS, BS)


def edge_lines(meta, keep, odd):
    place = lax.broadcasted_iota(jnp.int32, (16, BS), 0) == lax.broadcasted_iota(jnp.int32, (16, BS), 1)
    steps = lax.dot_general(
        meta, place.astype(jnp.bfloat16), (((0,), (0,)), ((), ())), preferred_element_type=jnp.float32
    )
    steps = jnp.where(odd, steps[:HALO], steps[1 : HALO + 1]).astype(jnp.int32)
    shift = jnp.where(odd, HALO + OWN, 0)
    row = lax.broadcasted_iota(jnp.int32, (HALO, BS), 0)
    lane = lax.broadcasted_iota(jnp.int32, (HALO, BS), 1)
    lines = jnp.full((HALO, BS), H_ZERO, jnp.int32)
    for b in range(KH):
        step = jnp.broadcast_to(steps[:, b : b + 1], (HALO, BS))
        col = jnp.where(step == 0, NO_COL, step + row + shift)
        hit = (col == lane) & (step != 0) & (keep != 0)
        lines = jnp.where(hit, row * KH + b, lines)
        w = col - (FIRST_COL - HALO)
        at = jnp.where(w < HALO, w + shift, jnp.where(w >= HALO + OWN, w - shift, w))
        at = jnp.where(step == 0, H_ROWS, at)
        lines = jnp.where(lane == COLS + b, at, lines)
    return lines


def stage(copies, passes, kind, coef, rest, *refs):
    n = len(copies)
    given, refs = refs[:1], refs[1:]
    arrived = refs[:n]
    ham, cheb, part, out, lines, table, meta, sems, table_sems = refs[-9:]
    first = kind == 0
    odd = (lax.axis_index("rows") & 1) == 1
    eye = (
        lax.broadcasted_iota(jnp.int32, (BS, BS), 0) == lax.broadcasted_iota(jnp.int32, (BS, BS), 1)
    ).astype(jnp.float32)
    c0, c1, c2, c3 = coef[0], coef[1], coef[2], coef[3]

    most = pltpu.make_async_copy(rest, table.at[pl.ds(HALO, LINES - HALO)], table_sems.at[0])
    most.start()
    if kind == 1:
        came = pltpu.make_async_copy(arrived[0].at[pl.ds(FIRST * KH * BS, 16)], meta, table_sems.at[1])
        came.start()
    moves = []
    for i, (rows, (even_from, odd_from), (even_at, odd_at)) in enumerate(copies):
        start = jnp.where(odd, odd_from, even_from) * KH
        at = jnp.where(odd, odd_at, even_at) * KH
        move = pltpu.make_async_copy(
            as_blocks(arrived[i]).at[pl.ds(start, rows * KH)], ham.at[pl.ds(at, rows * KH)], sems.at[i]
        )
        move.start()
        moves.append(move)
    if first:
        ham[H_ZERO] = jnp.zeros((BS, BS), jnp.bfloat16)
        cheb[T_ZERO] = jnp.zeros((BS, BS), jnp.bfloat16)
        lines[...] = jnp.full((HALO, BS), H_ZERO, jnp.int32)
    elif kind == 1:
        came.wait()
        lines[...] = edge_lines(meta[...], given[0][...], odd)
    else:
        lines[...] = given[0][...]
    far = pltpu.make_async_copy(lines, table.at[pl.ds(0, HALO)], table_sems.at[2])
    far.start()
    most.wait()
    far.wait()
    for move in moves:
        move.wait()

    def window_row(u):
        return jnp.where(odd, u + HALO + OWN - 1, HALO - u)

    def held_row(u):
        if u > 0:
            return jnp.where(odd, u - 1, HALO - u)
        if u <= -OWN:
            return jnp.where(odd, u + 2 * (HALO + OWN) - 1, HALO - u)
        return window_row(u)

    def term_row(u):
        w, at = window_row(u), held_row(u)
        j, r = w - REACH, w - HALO
        left = jnp.concatenate([ham[at * KH + b] for b in range(KH)], axis=1)
        bases = [table[at, COLS + b] for b in range(KH)]
        for group in range(KP // 4):
            cols = [table[T_LINES + j, COLS + group * 4 + t] for t in range(4)]
            right = jnp.concatenate(
                [jnp.concatenate([ham[table[base, q]] for q in cols], axis=1) for base in bases],
                axis=0,
            )
            total = jnp.dot(left, right, preferred_element_type=jnp.float32)
            for t in range(4):
                q = cols[t]
                on_diagonal = (q == w + (FIRST_COL - HALO)).astype(jnp.float32)
                value = 2.0 * total[:, t * BS : (t + 1) * BS] - on_diagonal * eye
                cheb[j * KP + group * 4 + t] = value.astype(jnp.bfloat16)
                if -OWN < u <= 0:
                    one = ham[table[at, q]].astype(jnp.float32)
                    part[r * KP + group * 4 + t] = (
                        c2 * value + (c1 - c3) * one + (c0 * on_diagonal) * eye
                    )

    sent = []

    def final_row(u):
        w = window_row(u)
        r = w - HALO
        left = jnp.concatenate([ham[w * KH + b] for b in range(KH)], axis=1)
        line = T_LINES + w - REACH
        bases = [table[line, COLS + KP + b] for b in range(KH)]
        for group in range(KP // 4):
            cols = [table[line, COLS + group * 4 + t] for t in range(4)]
            right = jnp.concatenate(
                [jnp.concatenate([cheb[table[base, q]] for q in cols], axis=1) for base in bases],
                axis=0,
            )
            total = jnp.dot(left, right, preferred_element_type=jnp.float32)
            for t in range(4):
                at = r * KP + group * 4 + t
                part[at] = part[at] + (2.0 * c3) * total[:, t * BS : (t + 1) * BS]
            some = pl.ds(r * KP + group * 4, 4)
            move = pltpu.make_async_copy(part.at[some], out.at[some], sems.at[n + len(sent)])
            move.start()
            sent.append(move)

    for term, low, high in passes:
        for u in range(low, high):
            if term == 2:
                term_row(u)
            else:
                final_row(u)
    for move in sent:
        move.wait()


def run_stage(copies, passes, kind, coefficients, rest, given, arrived, state):
    shapes = (
        pltpu.VMEM((H_ZERO + 1, BS, BS), jnp.bfloat16),
        pltpu.VMEM((T_ZERO + 1, BS, BS), jnp.bfloat16),
        pltpu.VMEM((OWN * KP, BS, BS), jnp.float32),
        jax.ShapeDtypeStruct((OWN * KP, BS, BS), jnp.float32),
        jax.ShapeDtypeStruct((HALO, BS), jnp.int32),
    )
    n = len(arrived)
    extra = [] if state is None else list(state[:4])
    work = sum(high - low for _, low, high in passes)
    sends = sum(high - low for term, low, high in passes if term == 3) * (KP // 4)
    return pl.pallas_call(
        functools.partial(stage, copies, passes, kind),
        out_shape=shapes,
        in_specs=[SMEM, ANY, VMEM] + [ANY] * n + [VMEM, VMEM, VMEM, ANY][: len(extra)],
        out_specs=(VMEM, VMEM, VMEM, ANY, VMEM),
        scratch_shapes=[
            pltpu.SMEM((LINES, BS), jnp.int32),
            pltpu.VMEM((16, BS), jnp.bfloat16),
            pltpu.SemaphoreType.DMA((n + sends,)),
            pltpu.SemaphoreType.DMA((3,)),
        ],
        input_output_aliases={3 + n + i: i for i in range(len(extra))},
        cost_estimate=pl.CostEstimate(
            flops=work * KH * KP * 2 * BS**3, bytes_accessed=work * KH * BS * BS * 2, transcendentals=0
        ),
        compiler_params=pltpu.CompilerParams(vmem_limit_bytes=8 << 20),
    )(coefficients, rest, given, *arrived, *extra)


def in_hbm(x):
    return pltpu.with_memory_space_constraint(x, pltpu.HBM)


def copy_edge(rows, even_from, odd_from, blocks, piece, sems):
    start = jnp.where((lax.axis_index("rows") & 1) == 1, odd_from, even_from) * (KH * BS)
    size = KH * BS
    return [
        pltpu.make_async_copy(
            blocks.at[pl.ds(start + i * size, size)], piece.at[pl.ds(i * size, size)], sems.at[i]
        )
        for i in range(rows)
    ]


def first_kernel(order_in, cols_in, blocks, piece, steps, order, cols, wide, sems):
    names = pltpu.make_async_copy(order_in, order, sems.at[FIRST])
    slots = pltpu.make_async_copy(cols_in, cols, sems.at[FIRST + 1])
    names.start()
    slots.start()
    moves = copy_edge(FIRST, 0, OWN - FIRST, blocks, piece, sems)
    for move in moves:
        move.start()
    names.wait()
    slots.wait()
    ids = cols[...]
    found = jnp.full(ids.shape, NO_COL, jnp.int32)
    for k in range(OWN + 2 * FIRST_COL):
        at = lax.axis_index("rows") * OWN + (k - FIRST_COL)
        inside = (at >= 0) & (at < order.shape[0])
        name = jnp.where(inside, order[jnp.clip(at, 0, order.shape[0] - 1)], -2)
        found = jnp.where(ids == name, k, found)
    row = lax.broadcasted_iota(jnp.int32, ids.shape, 1)
    step = jnp.where(found == NO_COL, 0, found - (row + (FIRST_COL - META)))
    steps[...] = step
    wide[...] = jnp.zeros_like(wide)
    wide[pl.ds(0, KH), pl.ds(0, OWN)] = step.astype(jnp.float32)
    piece[pl.ds(FIRST * KH * BS, 16)] = wide[...].astype(jnp.bfloat16)
    for move in moves:
        move.wait()


def pack_first(order, cols, blocks):
    size = FIRST * KH * BS
    return pl.pallas_call(
        first_kernel,
        out_shape=(pltpu.VMEM((size + 16, BS), jnp.bfloat16), jax.ShapeDtypeStruct((KH, OWN), jnp.int32)),
        in_specs=[ANY, ANY, ANY],
        out_specs=(VMEM, VMEM),
        scratch_shapes=[
            pltpu.SMEM(order.shape, jnp.int32),
            pltpu.VMEM((KH, OWN), jnp.int32),
            pltpu.VMEM((16, BS), jnp.float32),
            pltpu.SemaphoreType.DMA((FIRST + 2,)),
        ],
        cost_estimate=pl.CostEstimate(flops=0, bytes_accessed=size * BS * 2, transcendentals=0),
        compiler_params=pltpu.CompilerParams(vmem_limit_bytes=4 << 20),
    )(order, cols, blocks)


def second_kernel(blocks, after, piece, sems):
    moves = copy_edge(SECOND, FIRST, OWN - FIRST - SECOND, blocks, piece, sems)
    for move in moves:
        move.start()
    for move in moves:
        move.wait()


def pack_second(blocks, after):
    size = SECOND * KH * BS
    return pl.pallas_call(
        second_kernel,
        out_shape=pltpu.VMEM((size, BS), jnp.bfloat16),
        in_specs=[ANY, ANY],
        out_specs=VMEM,
        scratch_shapes=[pltpu.SemaphoreType.DMA((SECOND,))],
        cost_estimate=pl.CostEstimate(flops=0, bytes_accessed=size * BS * 2, transcendentals=0),
        compiler_params=pltpu.CompilerParams(vmem_limit_bytes=4 << 20),
    )(blocks, after)


def after_rows(first, last):
    return ((2, first - REACH, last - REACH + 1), (3, first - HALO, last - HALO + 1))


def columns_of(ids, order_window):
    found = ids[:, :, None] == order_window[None, None, :]
    places = jnp.arange(order_window.shape[0], dtype=jnp.int32) - NO_COL
    return jnp.sum(jnp.where(found, places[None, None, :], 0), axis=2) + NO_COL


def index_of(cols, first, spare, kept=None):
    rows, slots = cols.shape
    number = jnp.arange(rows * slots, dtype=jnp.int32).reshape(rows, slots, 1) + (first - spare)
    wanted = jnp.arange(COLS, dtype=jnp.int32)[None, None, :]
    hit = (cols[:, :, None] == wanted) & (wanted != NO_COL)
    if kept is not None:
        hit = hit & kept[:, None, :]
    return jnp.sum(jnp.where(hit, number, 0), axis=1) + spare


def local(order, ham_cols, dens_cols, ham_blocks, coefficients):
    axis = "rows"
    size = lax.axis_size(axis)
    me = lax.axis_index(axis)
    odd = (me & 1) == 1
    first_row = me * OWN
    near_pairs = [(i, i ^ 1) for i in range(size)]
    far_pairs = [(i, i + 1 if i % 2 else i - 1) for i in range(1, size - 1)]

    flat = in_hbm(ham_blocks.reshape(OWN * KH * BS, BS))
    blocks = ham_blocks.reshape(OWN * KH, BS, BS)
    piece_one, own_step = pack_first(in_hbm(order), in_hbm(ham_cols.T), flat)
    far_one = lax.ppermute(piece_one, axis, far_pairs)
    near_blocks = lax.ppermute(blocks, axis, near_pairs)
    near_step = lax.ppermute(own_step, axis, near_pairs)
    far_two = lax.ppermute(pack_second(flat, near_step), axis, far_pairs)

    order_window = lax.dynamic_slice_in_dim(
        jnp.pad(order, (FIRST_COL, FIRST_COL), constant_values=-2), first_row, OWN + 2 * FIRST_COL, 0
    )
    dens_window = lax.dynamic_slice_in_dim(
        jnp.pad(dens_cols, ((HALO, HALO), (0, 0)), constant_values=-1), first_row, H_ROWS, 0
    )
    all_cols = columns_of(dens_window, order_window)
    d_cols = all_cols[REACH : REACH + T_ROWS]
    wanted = jnp.arange(COLS, dtype=jnp.int32)[None, None, :]
    kept = jnp.any(all_cols[:, :, None] == wanted, axis=1)
    kept_near = jnp.where(odd, kept[:HALO], kept[HALO + OWN :])
    kept_far = jnp.where(odd, kept[HALO + OWN :], kept[:HALO])
    shift = (HALO + OWN) * odd.astype(jnp.int32)

    def columns(step, window):
        return jnp.where(step == 0, NO_COL, step + window)

    def lines_of(cols, first, keep):
        w = cols - (FIRST_COL - HALO)
        at = jnp.where(w < HALO, w + shift, jnp.where(w >= HALO + OWN, w - shift, w))
        named = jnp.where(cols == NO_COL, H_ROWS, at)
        lines = jnp.concatenate([index_of(cols, first * KH, H_ZERO, keep), named], axis=1)
        return jnp.pad(lines, ((0, 0), (0, LINE - COLS - KH)))

    steps = own_step.T
    own_cols = columns(steps, jnp.arange(OWN, dtype=jnp.int32)[:, None] + HALO)
    near_rows = jnp.arange(HALO, dtype=jnp.int32)[:, None] + (HALO + OWN) - shift
    near_steps = near_step.T
    near_cols = columns(jnp.where(odd, near_steps[1:], near_steps[:HALO]), near_rows)
    t_named = jnp.where(own_cols == NO_COL, T_ROWS, own_cols - (FIRST_COL - REACH)) + T_LINES
    t_lines = jnp.concatenate(
        [index_of(d_cols, 0, T_ZERO), d_cols, jnp.pad(t_named, ((REACH, REACH), (0, LINE - COLS - KP - KH)))],
        axis=1,
    )
    rest = jnp.concatenate(
        [
            lines_of(own_cols, HALO, kept[HALO : HALO + OWN]),
            lines_of(near_cols, HALO + OWN, kept_near),
            jnp.full((1, LINE), H_ZERO, jnp.int32),
            t_lines,
            jnp.full((1, LINE), T_ZERO, jnp.int32),
        ]
    )
    keep = jnp.pad(kept_far.astype(jnp.int32), ((0, 0), (0, LINE - COLS)))
    state = run_stage(
        ((OWN, (0, 0), (HALO, HALO)), (HALO, (0, 1), (HALO + OWN, HALO + OWN))),
        ((2, -3 * REACH, -REACH + 1), (3, -HALO, -HALO + 1)),
        0,
        coefficients,
        rest,
        keep,
        (in_hbm(blocks), near_blocks),
        None,
    )
    state = run_stage(
        ((FIRST, (0, 0), (HALO - FIRST, 0)),),
        after_rows(1, FIRST),
        1,
        coefficients,
        rest,
        keep,
        (far_one,),
        state,
    )
    state = run_stage(
        ((SECOND, (0, 0), (0, FIRST)),),
        after_rows(FIRST + 1, HALO),
        2,
        coefficients,
        rest,
        state[4],
        (far_two,),
        state,
    )
    return state[3].reshape(OWN, KP, BS, BS)


def solution(mesh):
    return jax.shard_map(
        local,
        mesh=mesh,
        in_specs=(P(), P("rows", None), P(), P("rows", None, None, None), P()),
        out_specs=P("rows", None, None, None),
        check_vma=False,
    )
```

time: 61.8 us -> 46 us (0.74)
  starting transfers between devices: 18.6 us -> 10.8 us
  waiting for transfers between devices: 3.47 us -> 0.01 us
  other arithmetic: 4.88 us -> 1.54 us
  local copies, waits for them, and re-layouts: 4.72 us -> 2.8 us
  Pallas kernels: 29.5 us -> 30.2 us
    ppermute x3 -> x2, starting transfers between devices: 18.1 us -> 10.3 us  [the longest x1 8.35 us: local(): far_one = lax.ppermute(piece_one, axis, far_pairs)]
    ppermute x3 -> x2, waiting for transfers between devices: 3.47 us -> 0.01 us  [the longest x1 0.01 us: local(): far_two = lax.ppermute(pack_second(flat, near_step), axis, far_pairs)]
    dynamic_slice x3 -> x1, local copies, waits for them, and re-layouts: 2.47 us -> 0.77 us  [local(): lax.dynamic_slice_in_dim(jnp.pad(order, (FIRST_COL, FIRST_COL), constant_...]
    select_n x2 -> x3, other arithmetic: 1.37 us -> 0.09 us  [the longest x2 0.08 us: lines_of(): named = jnp.where(cols == NO_COL, H_ROWS, at)]
    concatenate x1 -> x3, other arithmetic: 1.14 us -> 0.23 us  [the longest x2 0.15 us: lines_of(): jnp.concatenate([index_of(cols, first * KH, H_ZERO, keep), named], axis=1)]
    dynamic_slice x1 -> x0, other arithmetic: 0.77 us -> none  [local(): lax.dynamic_slice_in_dim(jnp.pad(order, (FIRST_COL, FIRST_COL), constant_...]
    dynamic_slice x2, local copies, waits for them, and re-layouts: 0.16 us -> 0.91 us  [local(): lax.dynamic_slice_in_dim(jnp.pad(dens_cols, ((HALO, HALO), (0, 0)), const...]
    pallas_call x4 -> x5, Pallas kernels: 29.5 us -> 30.2 us  [the longest x3 26.6 us: run_stage(): pl.pallas_call(functools.partial(stage, copies, passes, kind), out_shape=...]
  transfers between devices with their start and end apart: 5 -> 4, of which waited for: 1 -> 0; matrix products, arithmetic and copies ran while one was open for 12% -> 8% of each run, Pallas kernels for 43% -> 46%
where the time goes in v2:
time: 46 us; the launch traced here: 45.7 us
  Pallas kernels  30.2 us (66%)
  starting transfers between devices  10.8 us (23%)
  local copies, waits for them, and re-layouts  2.8 us (6%)
  other arithmetic  1.54 us (3%)
    pallas_call x3, Pallas kernels, run_stage(): pl.pallas_call(functools.partial(stage, copies, passes, kind), out_shape=...  26.6 us
    ppermute x1, starting transfers between devices, local(): far_one = lax.ppermute(piece_one, axis, far_pairs)  8.35 us
    pallas_call x1, Pallas kernels, pack_first(): pl.pallas_call(first_kernel, out_shape=(pltpu.VMEM((size + 16, BS), jnp.b...  2.41 us
    ppermute x1, starting transfers between devices, local(): far_two = lax.ppermute(pack_second(flat, near_step), axis, far_pairs)  1.92 us
    pallas_call x1, Pallas kernels, pack_second(): pl.pallas_call(second_kernel, out_shape=pltpu.VMEM((size, BS), jnp.bfloat...  1.13 us
  transfers between devices with their start and end apart: 4, of which 0 were waited for; matrix products, arithmetic and copies ran while one was open for 8% of the time, Pallas kernels for 46%

profile of v2, /device:TPU:6, one launch (start us, length us, event | category | flops | bytes accessed | tf_op | source)
XLA Modules:
  0.0 45.7 jit_solution(5573142272517270480)
XLA Ops:
  0.0 2.4 %shard_map.55 = (bf16[5136,128]{1,0:T(8,128)(2,1)}, s32[8,9]{1,0:T(8,128)S(1)}) custom-call(s32[1152]{0:T(1024)} %order_in.1, s32[8,9]{1,0:T(8,128)} %bitcast.13, bf16[9216,128]{1,0:T(8,128)(2,1)} %bitcast.8), custom_call_target="tpu_custom_call" | custom-call | bytes 1310720 | tf_op jit(solution)/shard_map/pallas_call | solution.py:248
  2.4 0.1 copy.19
  2.5 0.5 %collective-permute-start.2 = (bf16[72,128,128]{2,1,0:T(8,128)(2,1)}, bf16[72,128,128]{2,1,0:T(8,128)(2,1)}, u32[]{:S(2)}, u32[]{:S(2)}) collective-permute-start(bf16[72,128,128]{2,1,0:T(8,128)(2,1)} %bitcast.9), channel_id=1, source_target_pairs={{0,1},{1,0},{2,3},{3,2},{4,5},{5,4},{6,7},{7,6},{8,9},{9,8},{10,11... | collective-permute-start | bytes 7077896 | tf_op jit(solution)/shard_map/ppermute | solution.py:318
  3.0 8.3 %collective-permute-start.1 = (bf16[5136,128]{1,0:T(8,128)(2,1)}, bf16[5136,128]{1,0:T(8,128)(2,1)S(1)}, u32[]{:S(2)}, u32[]{:S(2)}) collective-permute-start(bf16[5136,128]{1,0:T(8,128)(2,1)} %get-tuple-element.18), channel_id=1, source_target_pairs={{1,2},{2,1},{3,4},{4,3},{5,6},{6,5},{7,8},{8,7},{9,10},{10,9},{11,... | collective-permute-start | bytes 3944456 | tf_op jit(solution)/shard_map/ppermute | solution.py:317
  11.4 0.8 %pad_dynamic-slice_fusion = s32[25,16]{0,1:T(8,128)S(1)} fusion(s32[]{:T(128)S(6)} %select_n.78, s32[1152,16]{0,1:T(8,128)} %param.7), kind=kLoop, calls=%fused_computation.6 | loop fusion | bytes 75332 | tf_op jit(solution)/shard_map/dynamic_slice | solution.py:325
  12.2 0.1 copy.21
  12.3 0.8 %pad_dynamic-slice_fusion.1 = s32[35]{0:T(128)S(1)} fusion(s32[]{:T(128)S(6)} %select_n.79, s32[1152]{0:T(1024)} %order_in.1), kind=kLoop, calls=%fused_computation.25 | loop fusion | bytes 4752 | tf_op jit(solution)/shard_map/dynamic_slice | solution.py:322
  13.1 0.6 %select_reduce_fusion = s32[25,16]{1,0:T(8,128)S(1)} fusion(s32[35]{0:T(128)S(1)} %iota_add_fusion, s32[35]{0:T(128)S(1)} %pad_dynamic-slice_fusion.1, s32[25,16]{1,0:T(8,128)S(1)} %copy.21), kind=kLoop, calls=%fused_computation.1 | loop fusion | flops 41600 | bytes 3480 | tf_op jit(solution)/shard_map/reduce_sum | solution.py:292
  13.7 0.1 fusion
  13.9 0.1 select_add_fusion
  14.0 0.1 select_reduce_fusion.2
  14.1 0.1 pad_add_fusion.1
  14.2 0.2 select_reduce_fusion.1
  14.4 0.1 pad_add_fusion
  14.5 0.1 fusion.9
  14.6 0.1 select_reduce_fusion.3
  14.8 0.1 copy.23.after
  14.9 1.1 %shard_map.58 = bf16[3072,128]{1,0:T(8,128)(2,1)S(1)} custom-call(bf16[9216,128]{1,0:T(8,128)(2,1)} %bitcast.10, s32[8,9]{1,0:T(8,128)S(1)} %copy.23.after), custom_call_target="tpu_custom_call" | custom-call | bytes 786432 | tf_op jit(solution)/shard_map/pallas_call | solution.py:274
  16.0 1.9 %collective-permute-start.3 = (bf16[3072,128]{1,0:T(8,128)(2,1)S(1)}, bf16[3072,128]{1,0:T(8,128)(2,1)S(1)}, u32[]{:S(2)}, u32[]{:S(2)}) collective-permute-start(bf16[3072,128]{1,0:T(8,128)(2,1)S(1)} %shard_map.58), channel_id=1, source_target_pairs={{1,2},{2,1},{3,4},{4,3},{5,6},{6,5},{7,8},{8,7},{9,10},{10,9},{11,... | collective-permute-start | bytes 2359304 | tf_op jit(solution)/shard_map/ppermute | solution.py:320
  18.0 0.3 concatenate.15.rest
  18.2 0.6 %copy-done = f32[4]{0:T(128)S(1)} copy-done((f32[4]{0:T(128)S(1)}, f32[4]{0:T(128)}, u32[]{:S(2)}) %copy-start) | copy-done | bytes 40
  18.9 10.8 %shard_map.56 = (bf16[201,128,128]{2,1,0:T(8,128)(2,1)S(1)}, bf16[273,128,128]{2,1,0:T(8,128)(2,1)S(1)}, f32[144,128,128]{2,1,0:T(8,128)S(1)}, f32[144,128,128]{2,1,0:T(8,128)}, s32[8,128]{1,0:T(8,128)}) custom-call(f32[4]{0:T(128)S(1)} %copy-done, s32[36,128]{1,0:T(8,128)S(1)} %concatenate.15.rest, s32[8,128]{1,0:T(8,128)S(1)} %pad_convert_fusion.refs_0_, ...), custom_call_target="tpu_custom_call" | custom-call | flops 5368709120 | bytes 2621440 | tf_op jit(solution)/shard_map/pallas_call | solution.py:185
  29.7 9.1 %shard_map.57 = (bf16[201,128,128]{2,1,0:T(8,128)(2,1)S(1)}, bf16[273,128,128]{2,1,0:T(8,128)(2,1)S(1)}, f32[144,128,128]{2,1,0:T(8,128)S(1)}, f32[144,128,128]{2,1,0:T(8,128)}, s32[8,128]{1,0:T(8,128)S(1)}) custom-call(f32[4]{0:T(128)S(1)} %copy-done, ...), custom_call_target="tpu_custom_call", output_to_operand_aliasing={{0}: (4, {}), {1}: (5, {}), {2}: (6, {}), {3}: (7, {})} | custom-call | flops 5368709120 | bytes 2621440 | tf_op jit(solution)/shard_map/pallas_call | solution.py:185
  38.8 6.7 %shard_map.59 = (bf16[201,128,128]{2,1,0:T(8,128)(2,1)S(1)}, bf16[273,128,128]{2,1,0:T(8,128)(2,1)S(1)}, f32[144,128,128]{2,1,0:T(8,128)S(1)}, f32[144,128,128]{2,1,0:T(8,128)}, s32[8,128]{1,0:T(8,128)}) custom-call(f32[4]{0:T(128)S(1)} %copy-done, ...), custom_call_target="tpu_custom_call", output_to_operand_aliasing={{0}: (4, {}), {1}: (5, {}), {2}: (6, {}), {3}: (7, {})} | custom-call | flops 3221225472 | bytes 1572864 | tf_op jit(solution)/shard_map/pallas_call | solution.py:185
  (27 shorter events, 0.2 us)
Async XLA Ops:
  2.5 12.0 %collective-permute-start = (s32[8,9]{0,1:T(8,128)S(1)}, s32[8,9]{0,1:T(8,128)S(1)}, u32[]{:S(2)}, u32[]{:S(2)}) collective-permute-start(s32[8,9]{0,1:T(8,128)S(1)} %copy.19), channel_id=1, source_target_pairs={{0,1},{1,0},{2,3},{3,2},{4,5},{5,4},{6,7},{7,6},{8,9},{9,8},{10,11... | collective-permute-start | bytes 872 | tf_op jit(solution)/shard_map/ppermute | solution.py:319
  2.5 15.7 %collective-permute-start.2 = (bf16[72,128,128]{2,1,0:T(8,128)(2,1)}, bf16[72,128,128]{2,1,0:T(8,128)(2,1)}, u32[]{:S(2)}, u32[]{:S(2)}) collective-permute-start(bf16[72,128,128]{2,1,0:T(8,128)(2,1)} %bitcast.9), channel_id=1, source_target_pairs={{0,1},{1,0},{2,3},{3,2},{4,5},{5,4},{6,7},{7,6},{8,9},{9,8},{10,11... | collective-permute-start | bytes 7077896 | tf_op jit(solution)/shard_map/ppermute | solution.py:318
  3.0 26.7 %collective-permute-start.1 = (bf16[5136,128]{1,0:T(8,128)(2,1)}, bf16[5136,128]{1,0:T(8,128)(2,1)S(1)}, u32[]{:S(2)}, u32[]{:S(2)}) collective-permute-start(bf16[5136,128]{1,0:T(8,128)(2,1)} %get-tuple-element.18), channel_id=1, source_target_pairs={{1,2},{2,1},{3,4},{4,3},{5,6},{6,5},{7,8},{8,7},{9,10},{10,9},{11,... | collective-permute-start | bytes 3944456 | tf_op jit(solution)/shard_map/ppermute | solution.py:317
  16.0 22.8 %collective-permute-start.3 = (bf16[3072,128]{1,0:T(8,128)(2,1)S(1)}, bf16[3072,128]{1,0:T(8,128)(2,1)S(1)}, u32[]{:S(2)}, u32[]{:S(2)}) collective-permute-start(bf16[3072,128]{1,0:T(8,128)(2,1)S(1)} %shard_map.58), channel_id=1, source_target_pairs={{1,2},{2,1},{3,4},{4,3},{5,6},{6,5},{7,8},{8,7},{9,10},{10,9},{11,... | collective-permute-start | bytes 2359304 | tf_op jit(solution)/shard_map/ppermute | solution.py:320
  18.2 0.7 %copy-start = (f32[4]{0:T(128)S(1)}, f32[4]{0:T(128)}, u32[]{:S(2)}) copy-start(f32[4]{0:T(128)} %coef.5) | copy-start | bytes 52

commit v3 on v2

--- a/solution.py
+++ b/solution.py
@@ -66,7 +66,7 @@
     n = len(copies)
     given, refs = refs[:1], refs[1:]
     arrived = refs[:n]
-    ham, cheb, part, out, lines, table, meta, sems, table_sems = refs[-9:]
+    ham, cheb, part, out, table, lines, made, meta, sems, table_sems = refs[-10:]
     first = kind == 0
     odd = (lax.axis_index("rows") & 1) == 1
     eye = (
@@ -74,8 +74,9 @@
     ).astype(jnp.float32)
     c0, c1, c2, c3 = coef[0], coef[1], coef[2], coef[3]
 
-    most = pltpu.make_async_copy(rest, table.at[pl.ds(HALO, LINES - HALO)], table_sems.at[0])
-    most.start()
+    if first:
+        most = pltpu.make_async_copy(rest, table.at[pl.ds(HALO, LINES - HALO)], table_sems.at[0])
+        most.start()
     if kind == 1:
         came = pltpu.make_async_copy(arrived[0].at[pl.ds(FIRST * KH * BS, 16)], meta, table_sems.at[1])
         came.start()
@@ -91,16 +92,14 @@
     if first:
         ham[H_ZERO] = jnp.zeros((BS, BS), jnp.bfloat16)
         cheb[T_ZERO] = jnp.zeros((BS, BS), jnp.bfloat16)
-        lines[...] = jnp.full((HALO, BS), H_ZERO, jnp.int32)
     elif kind == 1:
         came.wait()
         lines[...] = edge_lines(meta[...], given[0][...], odd)
-    else:
-        lines[...] = given[0][...]
-    far = pltpu.make_async_copy(lines, table.at[pl.ds(0, HALO)], table_sems.at[2])
-    far.start()
-    most.wait()
-    far.wait()
+        far = pltpu.make_async_copy(lines, table.at[pl.ds(0, HALO)], table_sems.at[2])
+        far.start()
+        far.wait()
+    if first:
+        most.wait()
     for move in moves:
         move.wait()
 
@@ -154,11 +153,12 @@
             total = jnp.dot(left, right, preferred_element_type=jnp.float32)
             for t in range(4):
                 at = r * KP + group * 4 + t
-                part[at] = part[at] + (2.0 * c3) * total[:, t * BS : (t + 1) * BS]
-            some = pl.ds(r * KP + group * 4, 4)
-            move = pltpu.make_async_copy(part.at[some], out.at[some], sems.at[n + len(sent)])
-            move.start()
-            sent.append(move)
+                made[len(sent) * KP + group * 4 + t] = part[at] + (2.0 * c3) * total[:, t * BS : (t + 1) * BS]
+        move = pltpu.make_async_copy(
+            made.at[pl.ds(len(sent) * KP, KP)], out.at[pl.ds(r * KP, KP)], sems.at[n + len(sent)]
+        )
+        move.start()
+        sent.append(move)
 
     for term, low, high in passes:
         for u in range(low, high):
@@ -176,28 +176,29 @@
         pltpu.VMEM((T_ZERO + 1, BS, BS), jnp.bfloat16),
         pltpu.VMEM((OWN * KP, BS, BS), jnp.float32),
         jax.ShapeDtypeStruct((OWN * KP, BS, BS), jnp.float32),
-        jax.ShapeDtypeStruct((HALO, BS), jnp.int32),
+        pltpu.SMEM((LINES, BS), jnp.int32),
     )
     n = len(arrived)
-    extra = [] if state is None else list(state[:4])
+    extra = [] if state is None else list(state)
     work = sum(high - low for _, low, high in passes)
-    sends = sum(high - low for term, low, high in passes if term == 3) * (KP // 4)
+    finals = sum(high - low for term, low, high in passes if term == 3)
     return pl.pallas_call(
         functools.partial(stage, copies, passes, kind),
         out_shape=shapes,
-        in_specs=[SMEM, ANY, VMEM] + [ANY] * n + [VMEM, VMEM, VMEM, ANY][: len(extra)],
-        out_specs=(VMEM, VMEM, VMEM, ANY, VMEM),
+        in_specs=[SMEM, ANY, VMEM] + [ANY] * n + [VMEM, VMEM, VMEM, ANY, SMEM][: len(extra)],
+        out_specs=(VMEM, VMEM, VMEM, ANY, SMEM),
         scratch_shapes=[
-            pltpu.SMEM((LINES, BS), jnp.int32),
+            pltpu.VMEM((HALO, BS), jnp.int32),
+            pltpu.VMEM((max(finals, 1) * KP, BS, BS), jnp.float32),
             pltpu.VMEM((16, BS), jnp.bfloat16),
-            pltpu.SemaphoreType.DMA((n + sends,)),
+            pltpu.SemaphoreType.DMA((n + finals,)),
             pltpu.SemaphoreType.DMA((3,)),
         ],
         input_output_aliases={3 + n + i: i for i in range(len(extra))},
         cost_estimate=pl.CostEstimate(
             flops=work * KH * KP * 2 * BS**3, bytes_accessed=work * KH * BS * BS * 2, transcendentals=0
         ),
-        compiler_params=pltpu.CompilerParams(vmem_limit_bytes=8 << 20),
+        compiler_params=pltpu.CompilerParams(vmem_limit_bytes=12 << 20),
     )(coefficients, rest, given, *arrived, *extra)
 
 
@@ -216,11 +217,13 @@
     ]
 
 
-def first_kernel(order_in, cols_in, blocks, piece, steps, order, cols, wide, sems):
+def first_kernel(order_in, cols_in, coef_in, blocks, piece, steps, window, coef, order, cols, wide, sems):
     names = pltpu.make_async_copy(order_in, order, sems.at[FIRST])
     slots = pltpu.make_async_copy(cols_in, cols, sems.at[FIRST + 1])
+    scales = pltpu.make_async_copy(coef_in, coef, sems.at[FIRST + 2])
     names.start()
     slots.start()
+    scales.start()
     moves = copy_edge(FIRST, 0, OWN - FIRST, blocks, piece, sems)
     for move in moves:
         move.start()
@@ -228,37 +231,47 @@
     slots.wait()
     ids = cols[...]
     found = jnp.full(ids.shape, NO_COL, jnp.int32)
+    lane = lax.broadcasted_iota(jnp.int32, window.shape, 1)
+    names_here = jnp.full(window.shape, -2, jnp.int32)
     for k in range(OWN + 2 * FIRST_COL):
         at = lax.axis_index("rows") * OWN + (k - FIRST_COL)
         inside = (at >= 0) & (at < order.shape[0])
         name = jnp.where(inside, order[jnp.clip(at, 0, order.shape[0] - 1)], -2)
         found = jnp.where(ids == name, k, found)
+        names_here = jnp.where(lane == k, name, names_here)
+    window[...] = names_here
     row = lax.broadcasted_iota(jnp.int32, ids.shape, 1)
     step = jnp.where(found == NO_COL, 0, found - (row + (FIRST_COL - META)))
     steps[...] = step
     wide[...] = jnp.zeros_like(wide)
     wide[pl.ds(0, KH), pl.ds(0, OWN)] = step.astype(jnp.float32)
     piece[pl.ds(FIRST * KH * BS, 16)] = wide[...].astype(jnp.bfloat16)
+    scales.wait()
     for move in moves:
         move.wait()
 
 
-def pack_first(order, cols, blocks):
+def pack_first(order, cols, coefficients, blocks):
     size = FIRST * KH * BS
     return pl.pallas_call(
         first_kernel,
-        out_shape=(pltpu.VMEM((size + 16, BS), jnp.bfloat16), jax.ShapeDtypeStruct((KH, OWN), jnp.int32)),
-        in_specs=[ANY, ANY, ANY],
-        out_specs=(VMEM, VMEM),
+        out_shape=(
+            pltpu.VMEM((size + 16, BS), jnp.bfloat16),
+            jax.ShapeDtypeStruct((KH, OWN), jnp.int32),
+            jax.ShapeDtypeStruct((8, BS), jnp.int32),
+            pltpu.SMEM(coefficients.shape, jnp.float32),
+        ),
+        in_specs=[ANY, ANY, ANY, ANY],
+        out_specs=(VMEM, VMEM, VMEM, SMEM),
         scratch_shapes=[
             pltpu.SMEM(order.shape, jnp.int32),
             pltpu.VMEM((KH, OWN), jnp.int32),
             pltpu.VMEM((16, BS), jnp.float32),
-            pltpu.SemaphoreType.DMA((FIRST + 2,)),
+            pltpu.SemaphoreType.DMA((FIRST + 3,)),
         ],
         cost_estimate=pl.CostEstimate(flops=0, bytes_accessed=size * BS * 2, transcendentals=0),
         compiler_params=pltpu.CompilerParams(vmem_limit_bytes=4 << 20),
-    )(order, cols, blocks)
+    )(order, cols, coefficients, blocks)
 
 
 def second_kernel(blocks, after, piece, sems):
@@ -313,15 +326,15 @@
 
     flat = in_hbm(ham_blocks.reshape(OWN * KH * BS, BS))
     blocks = ham_blocks.reshape(OWN * KH, BS, BS)
-    piece_one, own_step = pack_first(in_hbm(order), in_hbm(ham_cols.T), flat)
+    piece_one, own_step, window, scales = pack_first(
+        in_hbm(order), in_hbm(ham_cols.T), in_hbm(coefficients), flat
+    )
     far_one = lax.ppermute(piece_one, axis, far_pairs)
     near_blocks = lax.ppermute(blocks, axis, near_pairs)
     near_step = lax.ppermute(own_step, axis, near_pairs)
     far_two = lax.ppermute(pack_second(flat, near_step), axis, far_pairs)
 
-    order_window = lax.dynamic_slice_in_dim(
-        jnp.pad(order, (FIRST_COL, FIRST_COL), constant_values=-2), first_row, OWN + 2 * FIRST_COL, 0
-    )
+    order_window = window[0, : OWN + 2 * FIRST_COL]
     dens_window = lax.dynamic_slice_in_dim(
         jnp.pad(dens_cols, ((HALO, HALO), (0, 0)), constant_values=-1), first_row, H_ROWS, 0
     )
@@ -367,7 +380,7 @@
         ((OWN, (0, 0), (HALO, HALO)), (HALO, (0, 1), (HALO + OWN, HALO + OWN))),
         ((2, -3 * REACH, -REACH + 1), (3, -HALO, -HALO + 1)),
         0,
-        coefficients,
+        scales,
         rest,
         keep,
         (in_hbm(blocks), near_blocks),
@@ -377,7 +390,7 @@
         ((FIRST, (0, 0), (HALO - FIRST, 0)),),
         after_rows(1, FIRST),
         1,
-        coefficients,
+        scales,
         rest,
         keep,
         (far_one,),
@@ -387,9 +400,9 @@
         ((SECOND, (0, 0), (0, FIRST)),),
         after_rows(FIRST + 1, HALO),
         2,
-        coefficients,
+        scales,
         rest,
-        state[4],
+        keep,
         (far_two,),
         state,
     )

time: 46 us -> 41.2 us (0.90)
  Pallas kernels: 30.2 us -> 26.8 us
  local copies, waits for them, and re-layouts: 2.8 us -> 1.37 us
    pallas_call x3, Pallas kernels: 26.6 us -> 23.3 us  [run_stage(): pl.pallas_call(functools.partial(stage, copies, passes, kind), out_shape=...]
    dynamic_slice x1 -> x0, local copies, waits for them, and re-layouts: 0.77 us -> none  [local(): lax.dynamic_slice_in_dim(jnp.pad(order, (FIRST_COL, FIRST_COL), constant_...]
    unnamed x2 -> x0, local copies, waits for them, and re-layouts: 0.65 us -> none
  transfers between devices with their start and end apart: 4 -> 4, of which waited for: 0 -> 0; matrix products, arithmetic and copies ran while one was open for 8% -> 7% of each run, Pallas kernels for 46% -> 48%
where the time goes in v3:
time: 41.2 us; the launch traced here: 41 us
  Pallas kernels  26.8 us (65%)
  starting transfers between devices  10.8 us (26%)
  other arithmetic  1.55 us (4%)
  local copies, waits for them, and re-layouts  1.37 us (3%)
    pallas_call x3, Pallas kernels, run_stage(): pl.pallas_call(functools.partial(stage, copies, passes, kind), out_shape=...  23.3 us
    ppermute x1, starting transfers between devices, local(): far_one = lax.ppermute(piece_one, axis, far_pairs)  8.35 us
    pallas_call x1, Pallas kernels, pack_first(): pl.pallas_call(first_kernel, out_shape=(pltpu.VMEM((size + 16, BS), jnp.b...  2.42 us
    ppermute x1, starting transfers between devices, local(): far_two = lax.ppermute(pack_second(flat, near_step), axis, far_pairs)  1.92 us
    pallas_call x1, Pallas kernels, pack_second(): pl.pallas_call(second_kernel, out_shape=pltpu.VMEM((size, BS), jnp.bfloat...  1.13 us
    dynamic_slice x2, local copies, waits for them, and re-layouts, local(): lax.dynamic_slice_in_dim(jnp.pad(dens_cols, ((HALO, HALO), (0, 0)), const...  0.91 us
  transfers between devices with their start and end apart: 4, of which 0 were waited for; matrix products, arithmetic and copies ran while one was open for 7% of the time, Pallas kernels for 48%

profile of v3, /device:TPU:6, one launch (start us, length us, event | category | flops | bytes accessed | tf_op | source)
XLA Modules:
  0.0 41.0 jit_solution(968532856728998510)
XLA Ops:
  0.0 2.4 %shard_map.55 = (bf16[5136,128]{1,0:T(8,128)(2,1)}, s32[8,9]{1,0:T(8,128)S(1)}, s32[8,128]{1,0:T(8,128)S(1)}, f32[4]{0:T(128)S(4)}) custom-call(s32[1152]{0:T(1024)} %order_in.1, s32[8,9]{1,0:T(8,128)} %bitcast.15, f32[4]{0:T(128)} %coef_in.1, bf16[9216,128]{1,0:T(8,128)(2,1)} %bitcast.10), custom_call_target="tpu_custom_call" | custom-call | bytes 1310720 | tf_op jit(solution)/shard_map/pallas_call | solution.py:256
  2.4 0.1 copy.21
  2.5 0.0 collective-permute-start
  2.5 0.5 %collective-permute-start.3 = (bf16[72,128,128]{2,1,0:T(8,128)(2,1)}, bf16[72,128,128]{2,1,0:T(8,128)(2,1)}, u32[]{:S(2)}, u32[]{:S(2)}) collective-permute-start(bf16[72,128,128]{2,1,0:T(8,128)(2,1)} %bitcast.11), channel_id=1, source_target_pairs={{0,1},{1,0},{2,3},{3,2},{4,5},{5,4},{6,7},{7,6},{8,9},{9,8},{10,11... | collective-permute-start | bytes 7077896 | tf_op jit(solution)/shard_map/ppermute | solution.py:333
  3.0 8.3 %collective-permute-start.2 = (bf16[5136,128]{1,0:T(8,128)(2,1)}, bf16[5136,128]{1,0:T(8,128)(2,1)S(1)}, u32[]{:S(2)}, u32[]{:S(2)}) collective-permute-start(bf16[5136,128]{1,0:T(8,128)(2,1)} %get-tuple-element.23), channel_id=1, source_target_pairs={{1,2},{2,1},{3,4},{4,3},{5,6},{6,5},{7,8},{8,7},{9,10},{10,9},{11,... | collective-permute-start | bytes 3944456 | tf_op jit(solution)/shard_map/ppermute | solution.py:332
  11.4 0.8 %pad_dynamic-slice_fusion = s32[25,16]{0,1:T(8,128)S(1)} fusion(s32[]{:T(128)S(6)} %select_n.75, s32[1152,16]{0,1:T(8,128)} %param.7), kind=kLoop, calls=%fused_computation.6 | loop fusion | bytes 75332 | tf_op jit(solution)/shard_map/dynamic_slice | solution.py:338
  12.2 0.1 copy.23
  12.3 0.6 %select_reduce_fusion = s32[25,16]{1,0:T(8,128)S(1)} fusion(s32[35]{0:T(128)S(1)} %iota_add_fusion, s32[35]{0:T(128)S(1)} %slice_bitcast_fusion, s32[25,16]{1,0:T(8,128)S(1)} %copy.23), kind=kLoop, calls=%fused_computation.1 | loop fusion | flops 41600 | bytes 3480 | tf_op jit(solution)/shard_map/reduce_sum | solution.py:305
  13.0 0.1 fusion
  13.1 0.1 select_add_fusion
  13.2 0.1 select_reduce_fusion.2
  13.4 0.1 pad_add_fusion.1
  13.4 0.2 select_reduce_fusion.1
  13.6 0.1 pad_add_fusion
  13.8 0.1 fusion.9
  13.8 0.1 select_reduce_fusion.3
  13.9 0.1 pad_add_fusion.2
  14.0 0.1 copy.25.after
  14.1 1.1 %shard_map.56 = bf16[3072,128]{1,0:T(8,128)(2,1)S(1)} custom-call(bf16[9216,128]{1,0:T(8,128)(2,1)} %bitcast.12, s32[8,9]{1,0:T(8,128)S(1)} %copy.25.after), custom_call_target="tpu_custom_call" | custom-call | bytes 786432 | tf_op jit(solution)/shard_map/pallas_call | solution.py:287
  15.2 1.9 %collective-permute-start.1 = (bf16[3072,128]{1,0:T(8,128)(2,1)S(1)}, bf16[3072,128]{1,0:T(8,128)(2,1)S(1)}, u32[]{:S(2)}, u32[]{:S(2)}) collective-permute-start(bf16[3072,128]{1,0:T(8,128)(2,1)S(1)} %shard_map.56), channel_id=1, source_target_pairs={{1,2},{2,1},{3,4},{4,3},{5,6},{6,5},{7,8},{8,7},{9,10},{10,9},{11,... | collective-permute-start | bytes 2359304 | tf_op jit(solution)/shard_map/ppermute | solution.py:335
  17.2 0.3 concatenate.15.rest
  17.5 9.8 %shard_map.57 = (bf16[201,128,128]{2,1,0:T(8,128)(2,1)S(1)}, bf16[273,128,128]{2,1,0:T(8,128)(2,1)S(1)}, f32[144,128,128]{2,1,0:T(8,128)S(1)}, f32[144,128,128]{2,1,0:T(8,128)}, s32[44,128]{1,0:T(8,128)S(4)}) custom-call(f32[4]{0:T(128)S(4)} %get-tuple-element.20.coef, s32[36,128]{1,0:T(8,128)S(1)} %concatenate.15.rest, ...), custom_call_target="tpu_custom_call" | custom-call | flops 5368709120 | bytes 2621440 | tf_op jit(solution)/shard_map/pallas_call | solution.py:185
  27.3 8.5 %shard_map.58 = (bf16[201,128,128]{2,1,0:T(8,128)(2,1)S(1)}, bf16[273,128,128]{2,1,0:T(8,128)(2,1)S(1)}, f32[144,128,128]{2,1,0:T(8,128)S(1)}, f32[144,128,128]{2,1,0:T(8,128)}, s32[44,128]{1,0:T(8,128)S(4)}) custom-call(f32[4]{0:T(128)S(4)} %get-tuple-element.20.coef, ...), custom_call_target="tpu_custom_call", output_to_operand_aliasing={{0}: (4, {}), {1}: (5, {}), {2}: (6, {}), {3}: (7, {}), {4}... | custom-call | flops 5368709120 | bytes 2621440 | tf_op jit(solution)/shard_map/pallas_call | solution.py:185
  35.9 4.9 %shard_map.59 = (bf16[201,128,128]{2,1,0:T(8,128)(2,1)S(1)}, bf16[273,128,128]{2,1,0:T(8,128)(2,1)S(1)}, f32[144,128,128]{2,1,0:T(8,128)S(1)}, f32[144,128,128]{2,1,0:T(8,128)}, s32[44,128]{1,0:T(8,128)S(4)}) custom-call(f32[4]{0:T(128)S(4)} %get-tuple-element.20.coef, ...), custom_call_target="tpu_custom_call", output_to_operand_aliasing={{0}: (4, {}), {1}: (5, {}), {2}: (6, {}), {3}: (7, {}), {4}... | custom-call | flops 3221225472 | bytes 1572864 | tf_op jit(solution)/shard_map/pallas_call | solution.py:185
  (25 shorter events, 0.1 us)
Async XLA Ops:
  2.5 11.2 %collective-permute-start = (s32[8,9]{0,1:T(8,128)S(1)}, s32[8,9]{0,1:T(8,128)S(1)}, u32[]{:S(2)}, u32[]{:S(2)}) collective-permute-start(s32[8,9]{0,1:T(8,128)S(1)} %copy.21), channel_id=1, source_target_pairs={{0,1},{1,0},{2,3},{3,2},{4,5},{5,4},{6,7},{7,6},{8,9},{9,8},{10,11... | collective-permute-start | bytes 872 | tf_op jit(solution)/shard_map/ppermute | solution.py:334
  2.5 14.9 %collective-permute-start.3 = (bf16[72,128,128]{2,1,0:T(8,128)(2,1)}, bf16[72,128,128]{2,1,0:T(8,128)(2,1)}, u32[]{:S(2)}, u32[]{:S(2)}) collective-permute-start(bf16[72,128,128]{2,1,0:T(8,128)(2,1)} %bitcast.11), channel_id=1, source_target_pairs={{0,1},{1,0},{2,3},{3,2},{4,5},{5,4},{6,7},{7,6},{8,9},{9,8},{10,11... | collective-permute-start | bytes 7077896 | tf_op jit(solution)/shard_map/ppermute | solution.py:333
  3.0 24.3 %collective-permute-start.2 = (bf16[5136,128]{1,0:T(8,128)(2,1)}, bf16[5136,128]{1,0:T(8,128)(2,1)S(1)}, u32[]{:S(2)}, u32[]{:S(2)}) collective-permute-start(bf16[5136,128]{1,0:T(8,128)(2,1)} %get-tuple-element.23), channel_id=1, source_target_pairs={{1,2},{2,1},{3,4},{4,3},{5,6},{6,5},{7,8},{8,7},{9,10},{10,9},{11,... | collective-permute-start | bytes 3944456 | tf_op jit(solution)/shard_map/ppermute | solution.py:332
  15.2 20.6 %collective-permute-start.1 = (bf16[3072,128]{1,0:T(8,128)(2,1)S(1)}, bf16[3072,128]{1,0:T(8,128)(2,1)S(1)}, u32[]{:S(2)}, u32[]{:S(2)}) collective-permute-start(bf16[3072,128]{1,0:T(8,128)(2,1)S(1)} %shard_map.56), channel_id=1, source_target_pairs={{1,2},{2,1},{3,4},{4,3},{5,6},{6,5},{7,8},{8,7},{9,10},{10,9},{11,... | collective-permute-start | bytes 2359304 | tf_op jit(solution)/shard_map/ppermute | solution.py:335
